TPU v7x, 32 devices: a whole 2x2x4 slice. The times are simulated.
32 devices in a mesh: section: 4 (over x, core), dp: 8 (over z, y).
Axes of the slice: x: 2, y: 2, z: 4, core: 2. Of those that a mesh axis runs over, the one named last changes fastest.
Arguments:
- tokens: bfloat16 [4096, 1024], P('dp'), may hold values from -6 to 6
- segments: int32 [16, 256], P('dp'), may hold values from 0 to 4, never falling along the last dimension, each value on 1 to 96 neighbouring positions
- qkv_weight: bfloat16 [2048, 3072], P('section'), may hold values from -0.1875 to 0.1875
- qv_bias: bfloat16 [4096], P('section'), may hold values from -3 to 3
- out_weight: bfloat16 [2048, 1024], P('section'), may hold values from -1 to 1
- out_bias: bfloat16 [2048], P('section'), may hold values from -3 to 3
- up_weight: bfloat16 [2048, 4096], P('section'), may hold values from -0.1875 to 0.1875
- up_bias: bfloat16 [8192], P('section'), may hold values from -3 to 3
- down_weight: bfloat16 [8192, 1024], P('section'), may hold values from -0.125 to 0.125
- down_bias: bfloat16 [2048], P('section'), may hold values from -3 to 3
- norm_gain: float32 [4, 1024], P('section'), may hold values from 0.1 to 1.9
- norm_shift: float32 [4, 1024], P('section'), may hold values from -2 to 2
- cotangent: bfloat16 [4096, 1024], P('dp'), may hold values from -6 to 6
Outputs:
- block_output: bfloat16 [4096, 1024], P('dp', 'section')
- input_gradient: bfloat16 [4096, 1024], P('dp', 'section')
- grad_qkv_weight: float32 [2048, 3072], P(('section', 'dp'))
- grad_qv_bias: float32 [4096], P(('section', 'dp'))
- grad_out_weight: float32 [2048, 1024], P(('section', 'dp'))
- grad_out_bias: float32 [2048], P(('section', 'dp'))
- grad_up_weight: float32 [2048, 4096], P(('section', 'dp'))
- grad_up_bias: float32 [8192], P(('section', 'dp'))
- grad_down_weight: float32 [8192, 1024], P(('section', 'dp'))
- grad_down_bias: float32 [2048], P(('section', 'dp'))
- grad_norm_gain: float32 [4, 1024], P('section', 'dp')
- grad_norm_shift: float32 [4, 1024], P('section', 'dp')
Inputs may be any that keep to these rules, and one draw needn't show every extreme that they name: `segments`: segment numbers never fall along a row of 256 tokens; each of the 5 numbers appears in every row.
All inputs are finite; a program needn't handle non-finite values.
Results may differ from a plain program's by a relative error of at most 0.017.
Values may be sent and summed in bfloat16 or wider, within the bound.
No kernel may reach another device: no remote copies, remote signals or barrier semaphores. Data moves between devices by JAX's collectives and lax.ppermute only.
A program may use at most 640 MiB of HBM per device.

v0:
```python
import jax
import jax.numpy as jnp
from jax import lax
from jax.sharding import PartitionSpec as P

HEADS = 16
FF = 4096
ROW_LEN = 256
MICRO = 2
MB_ROWS = 1


EPSILON = 1e-06


def swapped(x, axis, apart):
    return lax.ppermute(x, axis, [(i, i ^ 1 << apart) for i in range(lax.axis_size(axis))])


def for_sending(x):
    return jax.tree.map(lambda a: a.astype(jnp.bfloat16) if a.dtype == jnp.float32 else a, x)


def from_behind(block, axis, distance):
    devices = range(lax.axis_size(axis))
    route = [(i - distance, i) for i in devices if i - distance in devices]
    return lax.ppermute(block, axis, route)


def broadcast(x, axis, root):
    mine = lax.axis_index(axis) == root
    return lax.psum(jnp.where(mine, x, jnp.zeros_like(x)), axis)


def layer_norm(values, gain_vector, shift_vector):
    center = values - jnp.mean(values, axis=-1, keepdims=True)
    spread = jnp.mean(center * center, axis=-1, keepdims=True)
    return center * lax.rsqrt(spread + EPSILON) * gain_vector + shift_vector


def gelu_exact(values):
    return jax.nn.gelu(values, approximate=False)


def store_slot(buffer, position, update, condition):
    current = lax.dynamic_index_in_dim(buffer, position, 0, False)
    return lax.dynamic_update_index_in_dim(
        buffer, jnp.where(condition, update, current), position, 0
    )


def attention_forward(entering, seg_ids, weight_set):
    qkv_full, qv_full, out_full, ob_full, gain_vector, shift_vector = weight_set
    token_count, model_width = entering.shape
    row_count, length = seg_ids.shape
    head_dim = model_width // HEADS
    score_scale = head_dim ** (-0.5)
    residual = entering.astype(jnp.float32)
    normed = layer_norm(residual, gain_vector, shift_vector).astype(jnp.bfloat16)
    projected = jnp.dot(normed, qkv_full, preferred_element_type=jnp.float32)
    biases = qv_full.astype(jnp.float32)
    queries = (
        (projected[:, :model_width] + biases[:model_width])
        .astype(jnp.bfloat16)
        .reshape(row_count, length, HEADS, head_dim)
    )
    key_rows = (
        projected[:, model_width : 2 * model_width]
        .astype(jnp.bfloat16)
        .reshape(row_count, length, HEADS, head_dim)
    )
    values = (
        (projected[:, 2 * model_width :] + biases[model_width:])
        .astype(jnp.bfloat16)
        .reshape(row_count, length, HEADS, head_dim)
    )
    scores = (
        jnp.einsum("rqhd,rkhd->rhqk", queries, key_rows, preferred_element_type=jnp.float32)
        * score_scale
    )
    allowed = (seg_ids[:, :, None] == seg_ids[:, None, :])[:, None]
    scores = jnp.where(allowed, scores, -1e30)
    row_max = jnp.max(scores, axis=-1, keepdims=True)
    exponent = jnp.exp(scores - row_max)
    softmax_weights = exponent / jnp.sum(exponent, axis=-1, keepdims=True)
    weights_low = softmax_weights.astype(jnp.bfloat16)
    attended = jnp.einsum(
        "rhqk,rkhd->rqhd", weights_low, values, preferred_element_type=jnp.float32
    )
    attended = attended.reshape(token_count, model_width).astype(jnp.bfloat16)
    branch = jnp.dot(attended, out_full, preferred_element_type=jnp.float32) + ob_full.astype(
        jnp.float32
    )
    result = (residual + branch).astype(jnp.bfloat16)
    return (
        result,
        (residual, normed, queries, key_rows, values, softmax_weights, weights_low, attended),
    )


def attention_backward(entering, seg_ids, grad_bf, weight_set):
    qkv_full, qv_full, out_full, ob_full, gain_vector, shift_vector = weight_set
    token_count, model_width = entering.shape
    row_count, length = seg_ids.shape
    head_dim = model_width // HEADS
    score_scale = head_dim ** (-0.5)
    result, stored = attention_forward(entering, seg_ids, weight_set)
    residual, normed, queries, key_rows, values, softmax_weights, weights_low, attended = stored
    grad_out = grad_bf.astype(jnp.float32)
    grad_wout = jnp.einsum("td,te->de", attended, grad_bf, preferred_element_type=jnp.float32)
    grad_bout = jnp.sum(grad_out, axis=0)
    grad_attended = jnp.einsum("te,de->td", grad_bf, out_full, preferred_element_type=jnp.float32)
    grad_attended = grad_attended.astype(jnp.bfloat16).reshape(row_count, length, HEADS, head_dim)
    grad_weights = jnp.einsum(
        "rqhd,rkhd->rhqk", grad_attended, values, preferred_element_type=jnp.float32
    )
    grad_values = jnp.einsum(
        "rhqk,rqhd->rkhd", weights_low, grad_attended, preferred_element_type=jnp.float32
    ).astype(jnp.bfloat16)
    grad_scores = softmax_weights * (
        grad_weights - jnp.sum(softmax_weights * grad_weights, axis=-1, keepdims=True)
    )
    grad_scores = grad_scores.astype(jnp.bfloat16)
    grad_queries = (
        jnp.einsum("rhqk,rkhd->rqhd", grad_scores, key_rows, preferred_element_type=jnp.float32)
        * score_scale
    ).astype(jnp.bfloat16)
    grad_keys = (
        jnp.einsum("rhqk,rqhd->rkhd", grad_scores, queries, preferred_element_type=jnp.float32)
        * score_scale
    ).astype(jnp.bfloat16)
    grad_queries = grad_queries.reshape(token_count, model_width)
    grad_keys = grad_keys.reshape(token_count, model_width)
    grad_values = grad_values.reshape(token_count, model_width)
    grad_joint = jnp.concatenate([grad_queries, grad_keys, grad_values], axis=1)
    grad_wqkv = jnp.einsum("td,te->de", normed, grad_joint, preferred_element_type=jnp.float32)
    grad_bias_q = jnp.sum(grad_queries.astype(jnp.float32), axis=0)
    grad_bias_v = jnp.sum(grad_values.astype(jnp.float32), axis=0)
    grad_normed = jnp.einsum("te,de->td", grad_joint, qkv_full, preferred_element_type=jnp.float32)
    unused_norm, pullback = jax.vjp(layer_norm, residual, gain_vector, shift_vector)
    grad_residual, grad_gain, grad_shift = pullback(grad_normed)
    grad_entering = (grad_out + grad_residual).astype(jnp.bfloat16)
    first_slab = jnp.concatenate([grad_wqkv, grad_wout], axis=1)
    second_slab = jnp.zeros((FF, model_width), jnp.float32)
    qv_pair = jnp.stack([grad_bias_q, grad_bias_v])
    out_pair = grad_bout.reshape(2, model_width // 2)
    up_pair = jnp.zeros((2, FF // 2), jnp.float32)
    return (
        grad_entering,
        first_slab,
        second_slab,
        qv_pair,
        out_pair,
        up_pair,
        grad_gain,
        grad_shift,
    )


def mlp_forward(entering, weight_set):
    up_full, ub_full, down_full, db_full, gain_vector, shift_vector = weight_set
    residual = entering.astype(jnp.float32)
    normed = layer_norm(residual, gain_vector, shift_vector).astype(jnp.bfloat16)
    hidden = jnp.dot(normed, up_full, preferred_element_type=jnp.float32) + ub_full.astype(
        jnp.float32
    )
    active = gelu_exact(hidden).astype(jnp.bfloat16)
    branch = jnp.dot(active, down_full, preferred_element_type=jnp.float32) + db_full.astype(
        jnp.float32
    )
    result = (residual + branch).astype(jnp.bfloat16)
    return (result, (residual, normed, hidden, active))


def mlp_backward(entering, grad_bf, weight_set):
    up_full, ub_full, down_full, db_full, gain_vector, shift_vector = weight_set
    model_width = entering.shape[1]
    result, stored = mlp_forward(entering, weight_set)
    residual, normed, hidden, active = stored
    grad_out = grad_bf.astype(jnp.float32)
    grad_wdown = jnp.einsum("tf,td->fd", active, grad_bf, preferred_element_type=jnp.float32)
    grad_bdown = jnp.sum(grad_out, axis=0)
    grad_active = jnp.einsum("td,fd->tf", grad_bf, down_full, preferred_element_type=jnp.float32)
    unused_gelu, gelu_back = jax.vjp(gelu_exact, hidden)
    grad_hidden = gelu_back(grad_active)[0].astype(jnp.bfloat16)
    grad_wup = jnp.einsum("td,tf->df", normed, grad_hidden, preferred_element_type=jnp.float32)
    grad_bup = jnp.sum(grad_hidden.astype(jnp.float32), axis=0)
    grad_normed = jnp.einsum("tf,df->td", grad_hidden, up_full, preferred_element_type=jnp.float32)
    unused_norm, pullback = jax.vjp(layer_norm, residual, gain_vector, shift_vector)
    grad_residual, grad_gain, grad_shift = pullback(grad_normed)
    grad_entering = (grad_out + grad_residual).astype(jnp.bfloat16)
    qv_pair = jnp.zeros((2, model_width), jnp.float32)
    out_pair = grad_bdown.reshape(2, model_width // 2)
    up_pair = grad_bup.reshape(2, FF // 2)
    return (grad_entering, grad_wup, grad_wdown, qv_pair, out_pair, up_pair, grad_gain, grad_shift)


def per_device(
    tokens,
    segments,
    qkv_weight,
    qv_bias,
    out_weight,
    out_bias,
    up_weight,
    up_bias,
    down_weight,
    down_bias,
    norm_gain,
    norm_shift,
    cotangent,
):
    model_width = tokens.shape[1]
    section_index = lax.axis_index("section")
    section_count = lax.axis_size("section")
    is_even = section_index % 2 == 0
    micro_size = MB_ROWS * ROW_LEN
    send_slab = jnp.where(is_even, up_weight, jnp.concatenate([qkv_weight, out_weight], axis=1))
    send_vector = jnp.concatenate([qv_bias, out_bias, up_bias, down_bias])
    part_slab, part_down, part_vector = swapped((send_slab, down_weight, send_vector), "section", 0)
    half_width = model_width // 2
    part_qv = part_vector[:model_width]
    part_ob = part_vector[model_width : model_width + half_width]
    part_ub = part_vector[model_width + half_width : model_width + half_width + FF // 2]
    part_db = part_vector[model_width + half_width + FF // 2 :]
    gain_vector = norm_gain[0]
    shift_vector = norm_shift[0]
    attention_set = (
        jnp.concatenate([qkv_weight, part_slab[:, : 3 * model_width]], axis=0),
        jnp.concatenate([qv_bias, part_qv]),
        jnp.concatenate([out_weight, part_slab[:, 3 * model_width :]], axis=0),
        jnp.concatenate([out_bias, part_ob]),
        gain_vector,
        shift_vector,
    )
    mlp_set = (
        jnp.concatenate([part_slab, up_weight], axis=0),
        jnp.concatenate([part_ub, up_bias]),
        jnp.concatenate([part_down, down_weight], axis=0),
        jnp.concatenate([part_db, down_bias]),
        gain_vector,
        shift_vector,
    )
    micro_tokens = tokens.reshape(MICRO, micro_size, model_width)
    micro_segs = segments.reshape(MICRO, MB_ROWS, ROW_LEN)
    micro_cot = cotangent.reshape(MICRO, micro_size, model_width)
    kept_inputs = jnp.zeros((MICRO, micro_size, model_width), jnp.bfloat16)
    finals = jnp.zeros((MICRO, micro_size, model_width), jnp.bfloat16)
    arriving = jnp.zeros((micro_size, model_width), jnp.bfloat16)
    moments = MICRO + section_count - 1
    for moment in range(moments):
        micro_index = moment - section_index
        is_valid = (micro_index >= 0) & (micro_index < MICRO)
        micro_slot = jnp.clip(micro_index, 0, MICRO - 1)
        entering = jnp.where(section_index == 0, micro_tokens[min(moment, MICRO - 1)], arriving)
        seg_now = lax.dynamic_index_in_dim(micro_segs, micro_slot, 0, False)
        branch_id = jnp.where(is_valid, jnp.where(is_even, 1, 2), 0)
        leaving = lax.switch(
            branch_id,
            [
                lambda: jnp.zeros_like(entering),
                lambda: attention_forward(entering, seg_now, attention_set)[0],
                lambda: mlp_forward(entering, mlp_set)[0],
            ],
        )
        kept_inputs = store_slot(kept_inputs, micro_slot, entering, is_valid)
        finals = store_slot(
            finals, micro_slot, leaving, is_valid & (section_index == section_count - 1)
        )
        if moment < moments - 1:
            arriving = jax.tree.map(
                lambda part, own: part.astype(own.dtype),
                from_behind(for_sending(leaving), "section", 1),
                leaving,
            )

    def spare_backward():
        return (
            jnp.zeros((micro_size, model_width), jnp.bfloat16),
            jnp.zeros((model_width, 4 * model_width), jnp.float32),
            jnp.zeros((FF, model_width), jnp.float32),
            jnp.zeros((2, model_width), jnp.float32),
            jnp.zeros((2, half_width), jnp.float32),
            jnp.zeros((2, FF // 2), jnp.float32),
            jnp.zeros((model_width,), jnp.float32),
            jnp.zeros((model_width,), jnp.float32),
        )

    totals = spare_backward()[1:]
    grad_inputs = jnp.zeros((MICRO, micro_size, model_width), jnp.bfloat16)
    arriving = jnp.zeros((micro_size, model_width), jnp.bfloat16)
    for moment in range(moments):
        micro_index = moment - (section_count - 1 - section_index)
        is_valid = (micro_index >= 0) & (micro_index < MICRO)
        micro_slot = jnp.clip(micro_index, 0, MICRO - 1)
        entering_grad = jnp.where(
            section_index == section_count - 1, micro_cot[min(moment, MICRO - 1)], arriving
        )
        seg_now = lax.dynamic_index_in_dim(micro_segs, micro_slot, 0, False)
        saved_input = lax.dynamic_index_in_dim(kept_inputs, micro_slot, 0, False)
        branch_id = jnp.where(is_valid, jnp.where(is_even, 1, 2), 0)
        results = lax.switch(
            branch_id,
            [
                spare_backward,
                lambda: attention_backward(saved_input, seg_now, entering_grad, attention_set),
                lambda: mlp_backward(saved_input, entering_grad, mlp_set),
            ],
        )
        leaving = results[0]
        totals = tuple(
            (first_term + second_term for first_term, second_term in zip(totals, results[1:]))
        )
        grad_inputs = store_slot(grad_inputs, micro_slot, leaving, is_valid & (section_index == 0))
        if moment < moments - 1:
            arriving = jax.tree.map(
                lambda part, own: part.astype(own.dtype),
                from_behind(for_sending(leaving), "section", -1),
                leaving,
            )
    first_slab, second_slab, qv_pair, out_pair, up_pair, gain_total, shift_total = totals
    slab_halves = first_slab.reshape(2, half_width, 4 * model_width)
    down_halves = second_slab.reshape(2, FF // 2, model_width)
    summed = (
        lax.psum_scatter(slab_halves, "dp", scatter_dimension=1, tiled=True),
        lax.psum_scatter(down_halves, "dp", scatter_dimension=1, tiled=True),
        lax.psum_scatter(qv_pair, "dp", scatter_dimension=1, tiled=True),
        lax.psum_scatter(out_pair, "dp", scatter_dimension=1, tiled=True),
        lax.psum_scatter(up_pair, "dp", scatter_dimension=1, tiled=True),
        lax.psum_scatter(gain_total[None], "dp", scatter_dimension=1, tiled=True),
        lax.psum_scatter(shift_total[None], "dp", scatter_dimension=1, tiled=True),
    )
    paired = summed[:5]
    kept_parts = tuple((jnp.where(is_even, halves[0], halves[1]) for halves in paired))
    sent_parts = tuple((jnp.where(is_even, halves[1], halves[0]) for halves in paired))
    arrived = swapped(
        (
            for_sending(sent_parts[0]),
            for_sending(sent_parts[1]),
            for_sending(sent_parts[2]),
            for_sending(sent_parts[3]),
            for_sending(sent_parts[4]),
        ),
        "section",
        0,
    )
    attention_rows = jnp.where(is_even, kept_parts[0], arrived[0])
    up_rows = jnp.where(is_even, arrived[0], kept_parts[0])
    down_rows = jnp.where(is_even, arrived[1], kept_parts[1])
    qv_rows = jnp.where(is_even, kept_parts[2], arrived[2])
    ob_rows = jnp.where(is_even, kept_parts[3], arrived[3])
    db_rows = jnp.where(is_even, arrived[3], kept_parts[3])
    ub_rows = jnp.where(is_even, arrived[4], kept_parts[4])
    gain_rows = summed[5]
    shift_rows = summed[6]
    quarter = model_width // section_count
    output_full = broadcast(
        finals.reshape(MICRO * micro_size, model_width), "section", section_count - 1
    )
    gradient_full = broadcast(grad_inputs.reshape(MICRO * micro_size, model_width), "section", 0)
    block_output = lax.dynamic_slice_in_dim(output_full, section_index * quarter, quarter, 1)
    input_gradient = lax.dynamic_slice_in_dim(gradient_full, section_index * quarter, quarter, 1)
    return (
        block_output,
        input_gradient,
        attention_rows[:, : 3 * model_width],
        qv_rows,
        attention_rows[:, 3 * model_width :],
        ob_rows,
        up_rows,
        ub_rows,
        down_rows,
        db_rows,
        gain_rows,
        shift_rows,
    )


def solution(mesh):
    placed = (
        P("dp", None),
        P("dp", None),
        P("section", None),
        P("section"),
        P("section", None),
        P("section"),
        P("section", None),
        P("section"),
        P("section", None),
        P("section"),
        P("section", None),
        P("section", None),
        P("dp", None),
    )
    return jax.shard_map(
        per_device,
        mesh=mesh,
        in_specs=placed,
        out_specs=(
            P("dp", "section"),
            P("dp", "section"),
            P(("section", "dp"), None),
            P(("section", "dp")),
            P(("section", "dp"), None),
            P(("section", "dp")),
            P(("section", "dp"), None),
            P(("section", "dp")),
            P(("section", "dp"), None),
            P(("section", "dp")),
            P("section", "dp"),
            P("section", "dp"),
        ),
        check_vma=False,
    )
```

profile of v0, /device:TPU:0, one launch (start us, length us, event | category | flops | bytes accessed | tf_op | source)
XLA Modules:
  0.0 1459.0 jit_solution(5213665342916188327)
XLA Ops:
  8.1 5.7 maximum_select_fusion
  15.6 5.4 collective-permute-done.1
  21.3 2.2 slice.368
  25.7 3.1 pad_maximum_fusion.25
  28.8 4.9 constant_dynamic-update-slice_fusion.1
  33.7 2.2 constant_dynamic-update-slice_fusion
  35.9 4.5 constant_dynamic-update-slice_fusion.3
  40.5 4.6 constant_dynamic-update-slice_fusion.2
  45.1 32.6 %conditional.10 = (bf16[256,1024]{1,0:T(8,128)(2,1)}) conditional(s32[]{:T(128)} %clamp.30, () %tuple.133, (bf16[256,1024]{1,0:T(8,128)(2,1)}, f32[1,1024]{1,0:T(1,128)S(1)}, f32[1,1024]{1,0:T(1,128)S(1)}, bf16[1024,3072]{1,0:T(8,128)(2,1)}, bf16[2048]{0:T(1024)(128)(2,1)S(1)}, /*index=5*/s32[2,256]{1,0:T(2,128)S(1)}, s32[]{:T(128)}, ...), branch_computations={%region_0.1_spmd, %region_1.6_spmd, %region_6.9_spmd} | conditional | flops 4368372736 | bytes 47405124 | solution.py:258
  47.6 4.9 fusion.16
  59.6 2.1 slice.490
  63.8 4.6 fusion.951
  68.4 2.9 fusion.7
  80.9 2.2 bitcast_dynamic-update-slice_fusion.8
  83.0 32.4 %conditional.11 = (bf16[256,1024]{1,0:T(8,128)(2,1)}) conditional(s32[]{:T(128)} %clamp.31, () %tuple.136, (bf16[256,1024]{1,0:T(8,128)(2,1)}, f32[1,1024]{1,0:T(1,128)S(1)}, f32[1,1024]{1,0:T(1,128)S(1)}, bf16[1024,3072]{1,0:T(8,128)(2,1)}, bf16[2048]{0:T(1024)(128)(2,1)S(1)}, /*index=5*/s32[2,256]{1,0:T(2,128)S(1)}, ...), branch_computations={%region_9.10_spmd, %region_10.15_spmd, %region_15.18_spmd} | conditional | flops 4368372736 | bytes 47405124 | solution.py:258
  85.6 4.9 fusion.139
  97.6 2.1 slice.491
  101.7 4.6 fusion.953
  106.3 2.9 fusion.130
  118.6 2.2 bitcast_dynamic-update-slice_fusion.7
  120.8 8.3 conditional.12
  129.1 17.6 %collective-permute-start.5 = (bf16[256,1024]{1,0:T(8,128)(2,1)}, bf16[256,1024]{1,0:T(8,128)(2,1)}, u32[]{:S(2)}, u32[]{:S(2)}) collective-permute-start(bf16[256,1024]{1,0:T(8,128)(2,1)} %get-tuple-element.1117), channel_id=1, source_target_pairs={{0,8},{8,16},{16,24},{1,9},{9,17},{17,25},{2,10},{10,18},{18,26},{... | collective-permute-start | bytes 1572872 | tf_op jit(solution)/shard_map/ppermute | solution.py:27
  147.8 2.2 bitcast_dynamic-update-slice_fusion.6
  149.9 3.9 conditional.13
  153.9 15.2 %collective-permute-start.6 = (bf16[256,1024]{1,0:T(8,128)(2,1)}, bf16[256,1024]{1,0:T(8,128)(2,1)}, u32[]{:S(2)}, u32[]{:S(2)}) collective-permute-start(bf16[256,1024]{1,0:T(8,128)(2,1)} %get-tuple-element.1118), channel_id=1, source_target_pairs={{0,8},{8,16},{16,24},{1,9},{9,17},{17,25},{2,10},{10,18},{18,26},{... | collective-permute-start | bytes 1572872 | tf_op jit(solution)/shard_map/ppermute | solution.py:27
  170.2 2.1 bitcast_dynamic-update-slice_fusion.5
  173.3 3.5 dynamic-slice_bitcast_fusion
  176.8 19.5 %conditional.15 = (bf16[256,1024]{1,0:T(8,128)(2,1)}, f32[1024,4096]{1,0:T(8,128)}, f32[4096,1024]{1,0:T(8,128)}, f32[2,1024]{1,0:T(2,128)S(1)}, f32[2,512]{1,0:...) conditional(s32[]{:T(128)} %clamp.35, () %tuple.148, ...), branch_computations={%region_46.47_spmd, %region_47.60_spmd, %region_60.69_spmd} | conditional | flops 10896537600 | bytes 209597792 | solution.py:302
  177.7 7.8 broadcast.2167
  185.5 7.8 broadcast.2168
  197.7 36.1 %collective-permute-done.7 = bf16[256,1024]{1,0:T(8,128)(2,1)S(1)} collective-permute-done((bf16[256,1024]{1,0:T(8,128)(2,1)}, bf16[256,1024]{1,0:T(8,128)(2,1)S(1)}, u32[]{:S(2)}, u32[]{:S(2)}) %collective-permute-start.7) | collective-permute-done | bytes 524320 | tf_op jit(solution)/shard_map/ppermute | solution.py:27
  234.9 19.3 %conditional.16 = (bf16[256,1024]{1,0:T(8,128)(2,1)}, f32[1024,4096]{1,0:T(8,128)}, f32[4096,1024]{1,0:T(8,128)}, f32[2,1024]{1,0:T(2,128)S(1)}, f32[2,512]{1,0:...) conditional(s32[]{:T(128)} %clamp.36, () %tuple.151, ...), branch_computations={%region_69.70_spmd, %region_70.83_spmd, %region_83.92_spmd} | conditional | flops 10896537600 | bytes 209597792 | solution.py:302
  235.8 7.8 broadcast.2216
  243.6 7.9 broadcast.2217
  255.7 10.0 collective-permute-done.8
  266.8 19.6 %conditional.17 = (bf16[256,1024]{1,0:T(8,128)(2,1)}, f32[1024,4096]{1,0:T(8,128)}, f32[4096,1024]{1,0:T(8,128)}, f32[2,1024]{1,0:T(2,128)S(1)}, f32[2,512]{1,0:...) conditional(s32[]{:T(128)} %clamp.37, () %tuple.154, ...), branch_computations={%region_92.93_spmd, %region_93.106_spmd, %region_106.115_spmd} | conditional | flops 10896537600 | bytes 209597792 | solution.py:302
  267.7 7.9 broadcast.2265
  275.6 7.8 broadcast.2266
  287.8 113.2 %collective-permute-done.9 = bf16[256,1024]{1,0:T(8,128)(2,1)S(1)} collective-permute-done((bf16[256,1024]{1,0:T(8,128)(2,1)}, bf16[256,1024]{1,0:T(8,128)(2,1)S(1)}, u32[]{:S(2)}, u32[]{:S(2)}) %collective-permute-start.9) | collective-permute-done | bytes 524320 | tf_op jit(solution)/shard_map/ppermute | solution.py:27
  402.2 67.8 %conditional.18 = (bf16[256,1024]{1,0:T(8,128)(2,1)}, f32[1024,4096]{1,0:T(8,128)}, f32[4096,1024]{1,0:T(8,128)}, f32[2,1024]{1,0:T(2,128)S(1)}, f32[2,512]{1,0:...) conditional(s32[]{:T(128)} %clamp.38, () %tuple.157, ...), branch_computations={%region_115.116_spmd, %region_116.129_spmd, %region_129.138_spmd} | conditional | flops 10896537600 | bytes 209597792 | solution.py:302
  407.2 4.7 fusion.837
  421.1 4.6 fusion.967
  425.7 3.9 convert_reduce_fusion.33
  431.7 3.5 multiply_reduce_fusion.3
  445.6 6.0 pad_maximum_fusion.15
  451.8 7.9 broadcast.2325
  471.4 7.7 collective-permute-done.10
  480.6 71.4 %conditional.19 = (bf16[256,1024]{1,0:T(8,128)(2,1)}, f32[1024,4096]{1,0:T(8,128)}, f32[4096,1024]{1,0:T(8,128)}, f32[2,1024]{1,0:T(2,128)S(1)}, f32[2,512]{1,0:...) conditional(s32[]{:T(128)} %clamp.39, () %tuple.160, ...), branch_computations={%region_138.139_spmd, %region_139.152_spmd, %region_152.161_spmd} | conditional | flops 10896537600 | bytes 205403424 | solution.py:302
  484.9 4.7 fusion.900
  498.8 4.6 fusion.969
  503.4 3.9 convert_reduce_fusion.40
  509.4 3.5 multiply_reduce_fusion.4
  523.3 6.0 pad_maximum_fusion.20
  529.5 7.8 broadcast.2374
  558.0 34.3 %add_add_fusion.11 = f32[1024,4096]{1,0:T(8,128)} fusion(f32[1024,4096]{1,0:T(8,128)} %get-tuple-element.761, f32[1024,4096]{1,0:T(8,128)} %get-tuple-element.760, f32[1024,4096]{1,0:T(8,128)} %get-tuple-element.759, f32[1024,4096]{1,0:T(8,128)} %get-tuple-element.757, f32[1024,4096]{1,0:T(8,128)} %get-tuple-element.758), kind=kLoop, calls=%fused_computation.1226 | loop fusion | flops 16777216 | bytes 100663296 | tf_op jit(solution)/shard_map/add | solution.py:312
  595.4 5.7 conditional.14
  601.4 2.1 bitcast_dynamic-update-slice_fusion.10
  607.6 35.7 %add_add_fusion.10 = f32[4096,1024]{1,0:T(8,128)} fusion(f32[4096,1024]{1,0:T(8,128)} %get-tuple-element.781, f32[4096,1024]{1,0:T(8,128)} %get-tuple-element.780, f32[4096,1024]{1,0:T(8,128)} %get-tuple-element.779, f32[4096,1024]{1,0:T(8,128)} %get-tuple-element.777, f32[4096,1024]{1,0:T(8,128)} %get-tuple-element.778), kind=kLoop, calls=%fused_computation.1225 | loop fusion | flops 16777216 | bytes 100663296 | tf_op jit(solution)/shard_map/add | solution.py:312
  644.5 36.4 %reduce-scatter.28.cloned.1.call-done = f32[128,1]{1,0:T(8,128)} async-done(((f32[1024,1]{1,0:T(8,128)}), f32[128,1]{1,0:T(8,128)}) %reduce-scatter.28.cloned.1.call-update) | async-done | bytes 528
  682.3 62.9 %reduce-scatter.30.cloned.1.call-done = f32[128,1]{1,0:T(8,128)} async-done(((f32[1024,1]{1,0:T(8,128)}), f32[128,1]{1,0:T(8,128)}) %reduce-scatter.30.cloned.1.call-update) | async-done | bytes 528
  746.6 63.1 %reduce-scatter.22.cloned.1.call-done = f32[128,2]{1,0:T(8,128)} async-done(((f32[1024,2]{1,0:T(8,128)}), f32[128,2]{1,0:T(8,128)}) %reduce-scatter.22.cloned.1.call-update) | async-done | bytes 1040
  812.5 62.9 %reduce-scatter.26.cloned.1.call-done = f32[256,2]{1,0:T(8,128)} async-done(((f32[2048,2]{1,0:T(8,128)}), f32[256,2]{1,0:T(8,128)}) %reduce-scatter.26.cloned.1.call-update) | async-done | bytes 2064
  876.8 283.7 %reduce-scatter.18.cloned.1.call-done = f32[2,64,4096]{2,1,0:T(8,128)} async-done(((f32[2,512,4096]{2,1,0:T(8,128)}), f32[2,64,4096]{2,1,0:T(8,128)}) %reduce-scatter.18.cloned.1.call-update) | async-done | bytes 2097168 | tf_op jit(solution)/shard_map/reduce_scatter | solution.py:325
  1166.2 278.9 %reduce-scatter.20.cloned.1.call-done = f32[2,256,1024]{2,1,0:T(8,128)} async-done(((f32[2,2048,1024]{2,1,0:T(8,128)}), f32[2,256,1024]{2,1,0:T(8,128)}) %reduce-scatter.20.cloned.1.call-update) | async-done | bytes 2097168 | tf_op jit(solution)/shard_map/reduce_scatter | solution.py:326
  (413 shorter events, 140.6 us)
Async XLA Ops:
  8.0 635.4 %reduce-scatter.24.cloned.1.call-start = ((), (), s32[]{:S(2)}) async-start(), calls=%async_computation.10 | async-start | bytes 294912
  13.8 7.5 collective-permute-start
  13.8 22.1 %collective-permute-start.2 = (bf16[2048,1024]{1,0:T(8,128)(2,1)}, bf16[2048,1024]{1,0:T(8,128)(2,1)}, u32[]{:S(2)}, u32[]{:S(2)}) collective-permute-start(bf16[2048,1024]{1,0:T(8,128)(2,1)} %param.51), channel_id=1, source_target_pairs={{0,8},{8,0},{16,24},{24,16},{1,9},{9,1},{17,25},{25,17},{2,10},{10... | collective-permute-start | bytes 12582920 | tf_op jit(solution)/shard_map/ppermute | solution.py:17
  14.3 6.6 collective-permute-start.1
  21.0 128.9 %copy-start.69 = (bf16[1024]{0:T(1024)(128)(2,1)}, bf16[1024]{0:T(1024)(128)(2,1)S(1)}, u32[]{:S(2)}) copy-start(bf16[1024]{0:T(1024)(128)(2,1)S(1)} %get-tuple-element.991) | copy-start | bytes 6148
  21.0 128.9 %copy-start.71 = (bf16[1024]{0:T(1024)(128)(2,1)}, bf16[1024]{0:T(1024)(128)(2,1)S(1)}, u32[]{:S(2)}) copy-start(bf16[1024]{0:T(1024)(128)(2,1)S(1)} %get-tuple-element.992) | copy-start | bytes 6148
  77.7 3.2 collective-permute-start.3
  115.5 3.2 collective-permute-start.4
  129.1 18.7 %collective-permute-start.5 = (bf16[256,1024]{1,0:T(8,128)(2,1)}, bf16[256,1024]{1,0:T(8,128)(2,1)}, u32[]{:S(2)}, u32[]{:S(2)}) collective-permute-start(bf16[256,1024]{1,0:T(8,128)(2,1)} %get-tuple-element.1117), channel_id=1, source_target_pairs={{0,8},{8,16},{16,24},{1,9},{9,17},{17,25},{2,10},{10,18},{18,26},{... | collective-permute-start | bytes 1572872 | tf_op jit(solution)/shard_map/ppermute | solution.py:27
  153.9 16.4 %collective-permute-start.6 = (bf16[256,1024]{1,0:T(8,128)(2,1)}, bf16[256,1024]{1,0:T(8,128)(2,1)}, u32[]{:S(2)}, u32[]{:S(2)}) collective-permute-start(bf16[256,1024]{1,0:T(8,128)(2,1)} %get-tuple-element.1118), channel_id=1, source_target_pairs={{0,8},{8,16},{16,24},{1,9},{9,17},{17,25},{2,10},{10,18},{18,26},{... | collective-permute-start | bytes 1572872 | tf_op jit(solution)/shard_map/ppermute | solution.py:27
  176.8 58.1 %copy-start.3 = (bf16[256,1024]{1,0:T(8,128)(2,1)S(1)}, bf16[256,1024]{1,0:T(8,128)(2,1)}, u32[]{:S(2)}) copy-start(bf16[256,1024]{1,0:T(8,128)(2,1)} %get-tuple-element.979) | copy-start | bytes 1572868
  196.3 38.6 %copy-start.73 = (f32[2,2048]{1,0:T(2,128)}, f32[2,2048]{1,0:T(2,128)S(1)}, u32[]{:S(2)}) copy-start(f32[2,2048]{1,0:T(2,128)S(1)} %get-tuple-element.772) | copy-start | bytes 49156
  196.3 38.6 %copy-start.82 = (f32[2,1024]{1,0:T(2,128)}, f32[2,1024]{1,0:T(2,128)S(1)}, u32[]{:S(2)}) copy-start(f32[2,1024]{1,0:T(2,128)S(1)} %get-tuple-element.762) | copy-start | bytes 24580
  196.4 38.6 %copy-start.90 = (f32[2,512]{1,0:T(2,128)}, f32[2,512]{1,0:T(2,128)S(1)}, u32[]{:S(2)}) copy-start(f32[2,512]{1,0:T(2,128)S(1)} %get-tuple-element.767) | copy-start | bytes 12292
  196.4 38.6 %copy-start.92 = (f32[1024]{0:T(1024)}, f32[1024]{0:T(1024)S(1)}, u32[]{:S(2)}) copy-start(f32[1024]{0:T(1024)S(1)} %get-tuple-element.782) | copy-start | bytes 12292
  196.4 38.6 %copy-start.94 = (f32[1024]{0:T(1024)}, f32[1024]{0:T(1024)S(1)}, u32[]{:S(2)}) copy-start(f32[1024]{0:T(1024)S(1)} %get-tuple-element.787) | copy-start | bytes 12292
  196.4 37.4 %collective-permute-start.7 = (bf16[256,1024]{1,0:T(8,128)(2,1)}, bf16[256,1024]{1,0:T(8,128)(2,1)S(1)}, u32[]{:S(2)}, u32[]{:S(2)}) collective-permute-start(bf16[256,1024]{1,0:T(8,128)(2,1)} %get-tuple-element.752), channel_id=1, source_target_pairs={{8,0},{16,8},{24,16},{9,1},{17,9},{25,17},{10,2},{18,10},{26,18},{... | collective-permute-start | bytes 1572872 | tf_op jit(solution)/shard_map/ppermute | solution.py:27
  234.9 31.9 %copy-start.2 = (bf16[256,1024]{1,0:T(8,128)(2,1)S(1)}, bf16[256,1024]{1,0:T(8,128)(2,1)}, u32[]{:S(2)}) copy-start(bf16[256,1024]{1,0:T(8,128)(2,1)} %get-tuple-element.978) | copy-start | bytes 1572868
  254.3 12.5 copy-start.75
  254.3 12.5 copy-start.84
  254.3 12.5 copy-start.96
  254.3 11.3 collective-permute-start.8
  266.8 135.4 %copy-start.1 = (bf16[256,1024]{1,0:T(8,128)(2,1)S(1)}, bf16[256,1024]{1,0:T(8,128)(2,1)}, u32[]{:S(2)}) copy-start(bf16[256,1024]{1,0:T(8,128)(2,1)} %get-tuple-element.977) | copy-start | bytes 1572868
  286.5 115.7 %copy-start.77 = (f32[2,2048]{1,0:T(2,128)}, f32[2,2048]{1,0:T(2,128)S(1)}, u32[]{:S(2)}) copy-start(f32[2,2048]{1,0:T(2,128)S(1)} %get-tuple-element.774) | copy-start | bytes 49156
  286.5 115.7 %copy-start.86 = (f32[2,1024]{1,0:T(2,128)}, f32[2,1024]{1,0:T(2,128)S(1)}, u32[]{:S(2)}) copy-start(f32[2,1024]{1,0:T(2,128)S(1)} %get-tuple-element.764) | copy-start | bytes 24580
  286.5 115.7 %copy-start.102 = (f32[2,512]{1,0:T(2,128)}, f32[2,512]{1,0:T(2,128)S(1)}, u32[]{:S(2)}) copy-start(f32[2,512]{1,0:T(2,128)S(1)} %get-tuple-element.769) | copy-start | bytes 12292
  286.5 115.7 %copy-start.104 = (f32[1024]{0:T(1024)}, f32[1024]{0:T(1024)S(1)}, u32[]{:S(2)}) copy-start(f32[1024]{0:T(1024)S(1)} %get-tuple-element.784) | copy-start | bytes 12292
  286.5 115.7 %copy-start.106 = (f32[1024]{0:T(1024)}, f32[1024]{0:T(1024)S(1)}, u32[]{:S(2)}) copy-start(f32[1024]{0:T(1024)S(1)} %get-tuple-element.789) | copy-start | bytes 12292
  286.5 114.5 %collective-permute-start.9 = (bf16[256,1024]{1,0:T(8,128)(2,1)}, bf16[256,1024]{1,0:T(8,128)(2,1)S(1)}, u32[]{:S(2)}, u32[]{:S(2)}) collective-permute-start(bf16[256,1024]{1,0:T(8,128)(2,1)} %get-tuple-element.754), channel_id=1, source_target_pairs={{8,0},{16,8},{24,16},{9,1},{17,9},{25,17},{10,2},{18,10},{26,18},{... | collective-permute-start | bytes 1572872 | tf_op jit(solution)/shard_map/ppermute | solution.py:27
  402.1 78.2 %copy-start = (bf16[256,1024]{1,0:T(8,128)(2,1)S(1)}, bf16[256,1024]{1,0:T(8,128)(2,1)}, u32[]{:S(2)}) copy-start(bf16[256,1024]{1,0:T(8,128)(2,1)} %get-tuple-element.976) | copy-start | bytes 1572868
  470.1 9.0 collective-permute-start.10
  480.4 71.6 %copy-start.91 = (f32[2,512]{1,0:T(2,128)S(1)}, f32[2,512]{1,0:T(2,128)}, u32[]{:S(2)}) copy-start(f32[2,512]{1,0:T(2,128)} %copy-done.90) | copy-start | bytes 12292
  480.4 71.6 %copy-start.97 = (f32[2,512]{1,0:T(2,128)S(1)}, f32[2,512]{1,0:T(2,128)}, u32[]{:S(2)}) copy-start(f32[2,512]{1,0:T(2,128)} %copy-done.96) | copy-start | bytes 12292
  480.4 71.6 %copy-start.103 = (f32[2,512]{1,0:T(2,128)S(1)}, f32[2,512]{1,0:T(2,128)}, u32[]{:S(2)}) copy-start(f32[2,512]{1,0:T(2,128)} %copy-done.102) | copy-start | bytes 12292
  480.4 71.6 %copy-start.109 = (f32[2,512]{1,0:T(2,128)S(1)}, f32[2,512]{1,0:T(2,128)}, u32[]{:S(2)}) copy-start(f32[2,512]{1,0:T(2,128)} %copy-done.108) | copy-start | bytes 12292
  480.4 72.5 %copy-start.93 = (f32[1024]{0:T(1024)S(1)}, f32[1024]{0:T(1024)}, u32[]{:S(2)}) copy-start(f32[1024]{0:T(1024)} %copy-done.92) | copy-start | bytes 12292
  480.4 72.5 %copy-start.99 = (f32[1024]{0:T(1024)S(1)}, f32[1024]{0:T(1024)}, u32[]{:S(2)}) copy-start(f32[1024]{0:T(1024)} %copy-done.98) | copy-start | bytes 12292
  480.5 72.5 %copy-start.105 = (f32[1024]{0:T(1024)S(1)}, f32[1024]{0:T(1024)}, u32[]{:S(2)}) copy-start(f32[1024]{0:T(1024)} %copy-done.104) | copy-start | bytes 12292
  480.5 72.5 %copy-start.111 = (f32[1024]{0:T(1024)S(1)}, f32[1024]{0:T(1024)}, u32[]{:S(2)}) copy-start(f32[1024]{0:T(1024)} %copy-done.110) | copy-start | bytes 12292
  480.5 73.6 %copy-start.95 = (f32[1024]{0:T(1024)S(1)}, f32[1024]{0:T(1024)}, u32[]{:S(2)}) copy-start(f32[1024]{0:T(1024)} %copy-done.94) | copy-start | bytes 12292
  480.5 73.6 %copy-start.101 = (f32[1024]{0:T(1024)S(1)}, f32[1024]{0:T(1024)}, u32[]{:S(2)}) copy-start(f32[1024]{0:T(1024)} %copy-done.100) | copy-start | bytes 12292
  480.5 73.6 %copy-start.107 = (f32[1024]{0:T(1024)S(1)}, f32[1024]{0:T(1024)}, u32[]{:S(2)}) copy-start(f32[1024]{0:T(1024)} %copy-done.106) | copy-start | bytes 12292
  480.5 73.6 %copy-start.113 = (f32[1024]{0:T(1024)S(1)}, f32[1024]{0:T(1024)}, u32[]{:S(2)}) copy-start(f32[1024]{0:T(1024)} %copy-done.112) | copy-start | bytes 12292
  480.5 74.8 %copy-start.83 = (f32[2,1024]{1,0:T(2,128)S(1)}, f32[2,1024]{1,0:T(2,128)}, u32[]{:S(2)}) copy-start(f32[2,1024]{1,0:T(2,128)} %copy-done.82) | copy-start | bytes 24580
  480.5 74.8 %copy-start.85 = (f32[2,1024]{1,0:T(2,128)S(1)}, f32[2,1024]{1,0:T(2,128)}, u32[]{:S(2)}) copy-start(f32[2,1024]{1,0:T(2,128)} %copy-done.84) | copy-start | bytes 24580
  480.5 74.8 %copy-start.87 = (f32[2,1024]{1,0:T(2,128)S(1)}, f32[2,1024]{1,0:T(2,128)}, u32[]{:S(2)}) copy-start(f32[2,1024]{1,0:T(2,128)} %copy-done.86) | copy-start | bytes 24580
  480.5 74.8 %copy-start.89 = (f32[2,1024]{1,0:T(2,128)S(1)}, f32[2,1024]{1,0:T(2,128)}, u32[]{:S(2)}) copy-start(f32[2,1024]{1,0:T(2,128)} %copy-done.88) | copy-start | bytes 24580
  480.6 75.9 %copy-start.74 = (f32[2,2048]{1,0:T(2,128)S(1)}, f32[2,2048]{1,0:T(2,128)}, u32[]{:S(2)}) copy-start(f32[2,2048]{1,0:T(2,128)} %copy-done.73) | copy-start | bytes 49156
  480.6 75.9 %copy-start.76 = (f32[2,2048]{1,0:T(2,128)S(1)}, f32[2,2048]{1,0:T(2,128)}, u32[]{:S(2)}) copy-start(f32[2,2048]{1,0:T(2,128)} %copy-done.75) | copy-start | bytes 49156
  480.6 75.9 %copy-start.78 = (f32[2,2048]{1,0:T(2,128)S(1)}, f32[2,2048]{1,0:T(2,128)}, u32[]{:S(2)}) copy-start(f32[2,2048]{1,0:T(2,128)} %copy-done.77) | copy-start | bytes 49156
  480.6 75.9 %copy-start.80 = (f32[2,2048]{1,0:T(2,128)S(1)}, f32[2,2048]{1,0:T(2,128)}, u32[]{:S(2)}) copy-start(f32[2,2048]{1,0:T(2,128)} %copy-done.79) | copy-start | bytes 49156
  552.9 128.0 %reduce-scatter.28.cloned.1.call-start = ((), (), s32[]{:S(2)}) async-start(), calls=%async_computation.12 | async-start | bytes 589824
  554.1 191.1 %reduce-scatter.30.cloned.1.call-start = ((), (), s32[]{:S(2)}) async-start(), calls=%async_computation.13 | async-start | bytes 589824
  555.2 254.4 %reduce-scatter.22.cloned.1.call-start = ((), (), s32[]{:S(2)}) async-start(), calls=%async_computation.9 | async-start | bytes 589824
  556.4 319.0 %reduce-scatter.26.cloned.1.call-start = ((), (), s32[]{:S(2)}) async-start(), calls=%async_computation.11 | async-start | bytes 1179648
  557.9 602.5 %reduce-scatter.18.cloned.1.call-start = ((), (), s32[]{:S(2)}) async-start(), calls=%async_computation.7 | async-start | bytes 18874368 | tf_op jit(solution)/shard_map/reduce_scatter | solution.py:325
  592.3 570.6 %all-reduce.3.cloned.1.call-start = ((), (), s32[]{:S(2)}) async-start(), calls=%async_computation.14 | async-start | bytes 4194304 | tf_op jit(solution)/shard_map/psum | solution.py:32
  607.6 837.6 %reduce-scatter.20.cloned.1.call-start = ((), (), s32[]{:S(2)}) async-start(), calls=%async_computation.8 | async-start | bytes 18874368 | tf_op jit(solution)/shard_map/reduce_scatter | solution.py:326
  644.5 166.4 %collective-permute-start.13 = (bf16[64]{0:T(256)(128)(2,1)S(1)}, bf16[64]{0:T(256)(128)(2,1)S(1)}, u32[]{:S(2)}, u32[]{:S(2)}) collective-permute-start(bf16[64]{0:T(256)(128)(2,1)S(1)} %fusion.939), channel_id=1, source_target_pairs={{0,8},{8,0},{16,24},{24,16},{1,9},{9,1},{17,25},{25,17},{2,10},{10... | collective-permute-start | bytes 392 | tf_op jit(solution)/shard_map/ppermute | solution.py:17
  810.8 1.2 collective-permute-start.12
  876.7 285.7 %collective-permute-start.14 = (bf16[256]{0:T(256)(128)(2,1)S(1)}, bf16[256]{0:T(256)(128)(2,1)S(1)}, u32[]{:S(2)}, u32[]{:S(2)}) collective-permute-start(bf16[256]{0:T(256)(128)(2,1)S(1)} %fusion.933), channel_id=1, source_target_pairs={{0,8},{8,0},{16,24},{24,16},{1,9},{9,1},{17,25},{25,17},{2,10},{10... | collective-permute-start | bytes 1544 | tf_op jit(solution)/shard_map/ppermute | solution.py:17
  1160.5 286.6 %copy-start.24 = (f32[2,64,4096]{2,1,0:T(8,128)S(1)}, f32[2,64,4096]{2,1,0:T(8,128)}, u32[]{:S(2)}) copy-start(f32[2,64,4096]{2,1,0:T(8,128)} %reduce-scatter.18.cloned.1.call-done) | copy-start | bytes 6291460
  1162.2 284.8 %collective-permute-start.11 = (bf16[64,4096]{1,0:T(8,128)(2,1)S(1)}, bf16[64,4096]{1,0:T(8,128)(2,1)S(1)}, u32[]{:S(2)}, u32[]{:S(2)}) collective-permute-start(bf16[64,4096]{1,0:T(8,128)(2,1)S(1)} %fusion.930), channel_id=1, source_target_pairs={{0,8},{8,0},{16,24},{24,16},{1,9},{9,1},{17,25},{25,17},{2,10},{10... | collective-permute-start | bytes 1572872 | tf_op jit(solution)/shard_map/ppermute | solution.py:17
  1447.0 2.9 collective-permute-start.15
  (52 other events, 212.0 us)
Sparse Core Ops, SparseCore 0:
  553.0 63.0 reduce-scatter.23
  619.8 61.0 reduce-scatter.27
  684.2 60.8 reduce-scatter.29
  748.7 60.9 reduce-scatter.21
  812.9 62.4 reduce-scatter.25
  879.5 280.9 reduce-scatter.17
  1164.2 280.9 reduce-scatter.19
Sparse Core Ops, SparseCore 1:
  607.7 53.1 all-reduce.2
where the time goes:
time: 1470 us; the launch traced here: 1460 us
  waiting for transfers between devices  964 us (66%)
  local copies, waits for them, and re-layouts  159 us (11%)
  other arithmetic  138 us (9%)
  matrix products  78 us (5%)
  loops' own time  59.3 us (4%)
  starting transfers between devices  43.4 us (3%)
  between operations  17.5 us (1%)
    reduce_scatter x1, waiting for transfers between devices, per_device(): lax.psum_scatter(slab_halves, 'dp', scatter_dimension=1, tiled=True)  284 us
    reduce_scatter x1, waiting for transfers between devices, per_device(): lax.psum_scatter(down_halves, 'dp', scatter_dimension=1, tiled=True)  279 us
    unnamed x13, waiting for transfers between devices  225 us
    ppermute x8, waiting for transfers between devices, from_behind(): return lax.ppermute(block, axis, route)  170 us
    add x7, other arithmetic, per_device(): first_term + second_term  70.1 us
    another operation x34, local copies, waits for them, and re-layouts  68.5 us
    ppermute x8, starting transfers between devices, from_behind(): return lax.ppermute(block, axis, route)  42.2 us
    another operation x5, loops' own time, per_device(): lax.switch(branch_id, [spare_backward, lambda: attention_backward(saved_i...  34.3 us
  transfers between devices with their start and end apart: 24, of which 16 were waited for; matrix products, arithmetic and copies ran while one was open for 8% of the time, Pallas kernels for 0%

commit v1 on v0

v1 whole, which is shorter than its diff:
```python
import jax
import jax.numpy as jnp
from jax import lax
from jax.sharding import PartitionSpec as P

HEADS = 16
ROW_LEN = 256
EPSILON = 1e-06
BF = jnp.bfloat16
F32 = jnp.float32


def layer_norm(values, gain_vector, shift_vector):
    center = values - jnp.mean(values, axis=-1, keepdims=True)
    spread = jnp.mean(center * center, axis=-1, keepdims=True)
    return center * lax.rsqrt(spread + EPSILON) * gain_vector + shift_vector


def core_swap(x):
    return lax.ppermute(x, "section", [(i, i ^ 1) for i in range(lax.axis_size("section"))])


def x_hop(x, pairs):
    return lax.ppermute(x, "section", pairs)


def y_swap(x):
    return lax.ppermute(x, "dp", [(i, i ^ 1) for i in range(lax.axis_size("dp"))])


def pick(x, index, axis=0):
    return lax.dynamic_index_in_dim(x, index, axis, keepdims=False)


def line_sum(blocks, place):
    count = blocks.shape[0]
    received = None
    total = pick(blocks, place).astype(F32)
    for step in range(count - 1):
        length = count - 1 - step
        rightward = place == step
        out = lax.dynamic_slice_in_dim(blocks, jnp.where(rightward, step + 1, 0), length, 0)
        if received is not None:
            part = lax.dynamic_slice_in_dim(received, jnp.where(rightward, 1, 0), length, 0)
            out = (out.astype(F32) + part.astype(F32)).astype(BF)
        pairs = []
        for source, target in ((step, step + 1), (count - 1 - step, count - 2 - step)):
            pairs += [(2 * source + y, 2 * target + y) for y in range(2)]
        received = lax.ppermute(out, "dp", pairs)
        from_left = place == step + 1
        total = total + pick(received, jnp.where(from_left, 0, length - 1)).astype(F32)
    return total


def sum_y_first(chunk, y, z):
    got = y_swap(pick(chunk, 1 - y, 1))
    mine = (pick(chunk, y, 1).astype(F32) + got.astype(F32)).astype(BF)
    return line_sum(mine, z)


def sum_z_first(chunk, y, z):
    mine = line_sum(chunk, z)
    got = y_swap(pick(mine, 1 - y).astype(BF))
    return pick(mine, y) + got.astype(F32)


def attention_forward(x, seg, w):
    w_qkv, b_qv, w_out, b_out, gain, shift = w
    d = x.shape[1]
    dh = d // HEADS
    r = x.astype(F32)
    a = layer_norm(r, gain, shift).astype(BF)
    joint = jnp.dot(a, w_qkv, preferred_element_type=F32)
    bias = jnp.concatenate([b_qv[:d], jnp.zeros_like(b_qv[:d]), b_qv[d:]])
    qkv = (joint + bias).astype(BF)
    q, k, v = (qkv[:, i * d : (i + 1) * d].reshape(-1, HEADS, dh) for i in range(3))
    p = softmax_of(q, k, seg)
    o = jnp.einsum("hqk,khd->qhd", p.astype(BF), v, preferred_element_type=F32)
    o = o.reshape(-1, d).astype(BF)
    y = (r + jnp.dot(o, w_out, preferred_element_type=F32) + b_out).astype(BF)
    return y, (x, a, qkv, o)


def softmax_of(q, k, seg):
    s = jnp.einsum("qhd,khd->hqk", q, k, preferred_element_type=F32) * q.shape[-1] ** -0.5
    s = jnp.where((seg[:, None] == seg[None, :])[None], s, -1e30)
    e = jnp.exp(s - jnp.max(s, axis=-1, keepdims=True))
    return e / jnp.sum(e, axis=-1, keepdims=True)


def norm_backward(x, da, gain, shift, g):
    _, pullback = jax.vjp(layer_norm, x.astype(F32), gain, shift)
    dr, dgain, dshift = pullback(da)
    return (g.astype(F32) + dr).astype(BF), dgain, dshift


def attention_backward(g, seg, saved, w):
    w_qkv, b_qv, w_out, b_out, gain, shift = w
    x, a, qkv, o = saved
    d = x.shape[1]
    dh = d // HEADS
    q, k, v = (qkv[:, i * d : (i + 1) * d].reshape(-1, HEADS, dh) for i in range(3))
    p = softmax_of(q, k, seg)
    do = lax.dot_general(g, w_out, (((1,), (1,)), ((), ())), preferred_element_type=F32)
    do = do.astype(BF).reshape(-1, HEADS, dh)
    dp = jnp.einsum("qhd,khd->hqk", do, v, preferred_element_type=F32)
    dv = jnp.einsum("hqk,qhd->khd", p.astype(BF), do, preferred_element_type=F32)
    ds = (p * (dp - jnp.sum(p * dp, axis=-1, keepdims=True))).astype(BF)
    scale = dh**-0.5
    dq = jnp.einsum("hqk,khd->qhd", ds, k, preferred_element_type=F32) * scale
    dk = jnp.einsum("hqk,qhd->khd", ds, q, preferred_element_type=F32) * scale
    dqkv = jnp.concatenate([m.reshape(-1, d).astype(BF) for m in (dq, dk, dv)], axis=1)
    da = lax.dot_general(dqkv, w_qkv, (((1,), (1,)), ((), ())), preferred_element_type=F32)
    return norm_backward(x, da, gain, shift, g) + (dqkv,)


def mlp_forward(x, w):
    w_up, b_up, w_down, b_down, gain, shift = w
    r = x.astype(F32)
    a = layer_norm(r, gain, shift).astype(BF)
    u = jnp.dot(a, w_up, preferred_element_type=F32) + b_up
    phi = 0.5 * (1.0 + lax.erf(u * 0.5**0.5))
    g = (u * phi).astype(BF)
    slope = (phi + u * jnp.exp(-0.5 * u * u) * (2 * jnp.pi) ** -0.5).astype(BF)
    y = (r + jnp.dot(g, w_down, preferred_element_type=F32) + b_down).astype(BF)
    return y, (x, a, g, slope)


def mlp_backward(g, saved, w):
    w_up, b_up, w_down, b_down, gain, shift = w
    x, a, act, slope = saved
    dg = lax.dot_general(g, w_down, (((1,), (1,)), ((), ())), preferred_element_type=F32)
    du = (dg * slope.astype(F32)).astype(BF)
    da = lax.dot_general(du, w_up, (((1,), (1,)), ((), ())), preferred_element_type=F32)
    return norm_backward(x, da, gain, shift, g) + (du,)


def weight_grad(left, right):
    return lax.dot_general(left, right, (((0,), (0,)), ((), ())), preferred_element_type=F32).astype(BF)


def per_device(
    tokens, segments, qkv_weight, qv_bias, out_weight, out_bias, up_weight, up_bias, down_weight, down_bias,
    norm_gain, norm_shift, cotangent,
):
    d = tokens.shape[1]
    ff = up_weight.shape[1]
    section = lax.axis_index("section")
    core, x = section % 2, section // 2
    dp = lax.axis_index("dp")
    y, z = dp % 2, dp // 2
    zs = lax.axis_size("dp") // 2
    later = x == 1
    fwd_pairs, bwd_pairs = [(0, 2), (1, 3)], [(2, 0), (3, 1)]

    vec = jnp.concatenate(
        [m.astype(F32).reshape(-1) for m in (qv_bias, out_bias, up_bias, down_bias, norm_gain, norm_shift)]
    )
    vec_got = core_swap(vec)
    qkv_got = core_swap(qkv_weight)
    out_got = core_swap(out_weight)
    up_got = core_swap(up_weight)
    down_got = core_swap(down_weight)

    def natural(own, got):
        return jnp.where(core == 0, jnp.concatenate([own, got]), jnp.concatenate([got, own]))

    sizes = [qv_bias.shape[0], out_bias.shape[0], up_bias.shape[0], down_bias.shape[0], d, d]
    parts, at = [], 0
    for size in sizes:
        parts.append(natural(vec[at : at + size], vec_got[at : at + size]))
        at += size
    b_qv, b_out, b_up, b_down, gains, shifts = parts
    w_attn = (natural(qkv_weight, qkv_got), b_qv, natural(out_weight, out_got), b_out, gains[:d], shifts[:d])
    w_mlp = (natural(up_weight, up_got), b_up, natural(down_weight, down_got), b_down, gains[d:], shifts[d:])

    rows = lambda m: pick(m.reshape(2, ROW_LEN, d), core)
    own_tokens, own_cot = rows(tokens), rows(cotangent)
    seg = pick(segments, core)

    r1, _ = attention_forward(own_tokens, seg, w_attn)
    r2, _ = mlp_forward(r1, w_mlp)
    hopped = x_hop(r2, fwd_pairs)
    entering = jnp.where(later, hopped, own_tokens)
    r1, saved_attn = attention_forward(entering, seg, w_attn)
    r2, saved_mlp = mlp_forward(r1, w_mlp)

    g1 = mlp_backward(own_cot, saved_mlp, w_mlp)[0]
    g0 = attention_backward(g1, seg, saved_attn, w_attn)[0]
    hopped = x_hop(g0, bwd_pairs)
    g_mlp = jnp.where(later, own_cot, hopped)

    def half(m, index):
        return pick(m.reshape(m.shape[0], 2, -1), index, 1)

    def both_rows(m):
        return jnp.concatenate([m, core_swap(m)])

    def both_halves(m):
        return jnp.concatenate([half(m, core), core_swap(half(m, 1 - core))])

    def blocks(m):
        return m.reshape((zs, 2, m.shape[0] // (2 * zs)) + m.shape[1:])

    act_all = both_halves(saved_mlp[2])
    a_mlp_all = both_halves(saved_mlp[1])
    o_all = both_halves(saved_attn[3])
    a_attn_all = both_halves(saved_attn[1])

    d_down = weight_grad(act_all, both_rows(g_mlp))
    down_a = sum_z_first(blocks(d_down[:, : d // 2]), y, z)
    down_b = sum_y_first(blocks(d_down[:, d // 2 :]), y, z)
    g_attn, dgain_mlp, dshift_mlp, du = mlp_backward(g_mlp, saved_mlp, w_mlp)
    d_up = weight_grad(a_mlp_all, both_rows(du))
    up_a = sum_y_first(blocks(d_up[:, : ff // 2]), y, z)
    up_b = sum_y_first(blocks(d_up[:, ff // 2 :]), y, z)
    d_out = weight_grad(o_all, both_rows(g_attn))
    g_in, dgain_attn, dshift_attn, dqkv = attention_backward(g_attn, seg, saved_attn, w_attn)
    d_qkv = weight_grad(a_attn_all, both_rows(dqkv))
    qkv_a = sum_y_first(blocks(d_qkv[:, : 2 * d]), y, z)
    qkv_b = sum_y_first(blocks(jnp.concatenate([d_qkv[:, 2 * d :], d_out], axis=1)), y, z)

    total = lambda m: jnp.sum(m.astype(F32), axis=0)
    dq_sum = total(dqkv)
    pieces = [
        jnp.concatenate([dq_sum[:d], dq_sum[2 * d :]]),
        total(g_attn),
        total(du),
        total(g_mlp),
        jnp.concatenate([dgain_attn, dgain_mlp]),
        jnp.concatenate([dshift_attn, dshift_mlp]),
    ]
    n_dp = 2 * zs
    small = jnp.concatenate([m.reshape(2, n_dp, -1) for m in pieces], axis=2)
    small = pick(small, core) + core_swap(pick(small, 1 - core))
    small = lax.psum_scatter(small.reshape(-1), "dp", scatter_dimension=0, tiled=True)
    vectors, at = [], 0
    for m in pieces:
        width = m.shape[0] // (2 * n_dp)
        vectors.append(small[at : at + width])
        at += width
    g_qv, g_out_b, g_up_b, g_down_b, g_gain, g_shift = vectors

    def columns(here, there, keep_side):
        mine = jnp.where(keep_side, here, there)
        own, other = half(mine, core), core_swap(half(mine, 1 - core))
        return jnp.where(core == 0, jnp.concatenate([own, other]), jnp.concatenate([other, own]))

    crossing = jnp.where(later, r2[:, : d // 2], g_in[:, d // 2 :])
    crossed = x_hop(crossing, fwd_pairs + bwd_pairs)
    block_output = columns(r2[:, d // 2 :], crossed, later)
    input_gradient = columns(g_in[:, : d // 2], crossed, jnp.logical_not(later))
    return (
        block_output,
        input_gradient,
        jnp.concatenate([qkv_a, qkv_b[:, :d]], axis=1),
        g_qv,
        qkv_b[:, d:],
        g_out_b,
        jnp.concatenate([up_a, up_b], axis=1),
        g_up_b,
        jnp.concatenate([down_a, down_b], axis=1),
        g_down_b,
        g_gain[None],
        g_shift[None],
    )


def solution(mesh):
    placed = (
        P("dp", None), P("dp", None), P("section", None), P("section"), P("section", None), P("section"),
        P("section", None), P("section"), P("section", None), P("section"), P("section", None), P("section", None),
        P("dp", None),
    )
    both = ("section", "dp")
    return jax.shard_map(
        per_device,
        mesh=mesh,
        in_specs=placed,
        out_specs=(
            P("dp", "section"), P("dp", "section"), P(both, None), P(both), P(both, None), P(both), P(both, None),
            P(both), P(both, None), P(both), P("section", "dp"), P("section", "dp"),
        ),
        check_vma=False,
    )
```

time: 1470 us -> 460 us (0.31)
  waiting for transfers between devices: 964 us -> 122 us
  local copies, waits for them, and re-layouts: 159 us -> 40.8 us
  other arithmetic: 138 us -> 30.1 us
  matrix products: 78 us -> 157 us
  loops' own time: 59.3 us -> 0 us
  blocking collectives: 0 us -> 37.4 us
  starting transfers between devices: 43.4 us -> 61.1 us
    reduce_scatter x2 -> x0, waiting for transfers between devices: 563 us -> none  [the longest x1 284 us: per_device(): lax.psum_scatter(slab_halves, 'dp', scatter_dimension=1, tiled=True)]
    unnamed x13 -> x0, waiting for transfers between devices: 225 us -> none
    dot_general x26 -> x28, matrix products: 59.6 us -> 150 us  [the longest x2 26.9 us: mlp_backward(): lax.dot_general(du, w_up, (((1,), (1,)), ((), ())), preferred_element_typ...]
    add x7 -> x8, other arithmetic: 70.1 us -> 1.01 us  [the longest x6 0.93 us: line_sum(): total + pick(received, jnp.where(from_left, 0, length - 1)).astype(F32)]
    another operation x38 -> x1, local copies, waits for them, and re-layouts: 68.8 us -> 0.01 us
    another operation x10 -> x0, loops' own time: 59.3 us -> none  [the longest x5 34.3 us: per_device(): lax.switch(branch_id, [spare_backward, lambda: attention_backward(saved_i...]
    ppermute x16 -> x43, waiting for transfers between devices: 176 us -> 122 us  [the longest x18 65.3 us: line_sum(): received = lax.ppermute(out, 'dp', pairs)]
    unnamed x0 -> x1, blocking collectives: none -> 37.4 us
  transfers between devices with their start and end apart: 24 -> 43, of which waited for: 16 -> 13; matrix products, arithmetic and copies ran while one was open for 8% -> 31% of each run, Pallas kernels for 0% -> 0%
where the time goes in v1:
time: 460 us; the launch traced here: 452 us
  matrix products  157 us (34%)
  waiting for transfers between devices  122 us (27%)
  starting transfers between devices  61.1 us (13%)
  local copies, waits for them, and re-layouts  40.8 us (9%)
  blocking collectives  37.4 us (8%)
  other arithmetic  30.1 us (7%)
    ppermute x18, waiting for transfers between devices, line_sum(): received = lax.ppermute(out, 'dp', pairs)  65.3 us
    ppermute x6, waiting for transfers between devices, y_swap(): lax.ppermute(x, 'dp', [(i, i ^ 1) for i in range(lax.axis_size('dp'))])  46.3 us
    ppermute x18, starting transfers between devices, line_sum(): received = lax.ppermute(out, 'dp', pairs)  41.8 us
    unnamed x1, blocking collectives  37.4 us
    dot_general x2, matrix products, mlp_backward(): lax.dot_general(du, w_up, (((1,), (1,)), ((), ())), preferred_element_typ...  26.9 us
    dot_general x2, matrix products, mlp_forward(): y = (r + jnp.dot(g, w_down, preferred_element_type=F32) + b_down).astype(BF)  25.4 us
    dot_general x4, matrix products, weight_grad(): lax.dot_general(left, right, (((0,), (0,)), ((), ())), preferred_element_...  17.3 us
    dot_general x2, matrix products, attention_backward(): lax.dot_general(dqkv, w_qkv, (((1,), (1,)), ((), ())), preferred_element_...  17.2 us
  transfers between devices with their start and end apart: 43, of which 13 were waited for; matrix products, arithmetic and copies ran while one was open for 31% of the time, Pallas kernels for 0%

profile of v1, /device:TPU:0, one launch (start us, length us, event | category | flops | bytes accessed | tf_op | source)
XLA Modules:
  0.0 451.9 jit_solution(15790162873409423067)
XLA Ops:
  7.5 1.3 fusion.90
  12.7 6.3 %fusion.12 = bf16[256,3072]{1,0:T(8,128)(2,1)S(1)} fusion(f32[3072]{0:T(1024)S(1)} %pad_maximum_fusion.5, f32[1024]{0:T(1024)S(1)} %get-tuple-element.66, f32[1024]{0:T(1024)S(1)} %get-tuple-element.67, f32[256]{0:T(256)S(1)} %add_rsqrt_fusion.1, f32[256]{0:T(256)S(1)} %broadcast_multiply_fusion.3, bf16[2,256,1024]{2,1,0:T(8,128)(2,1)} %bitcast.220, ...), kind=kOutput, calls=%fused_computation.37 | convolution fusion | flops 1642070016 | bytes 8411141 | tf_op jit(solution)/shard_map/dot_general | solution.py:73
  19.7 3.5 fusion.184
  23.3 2.8 fusion.71
  26.1 2.7 convert_reduce_fusion.4
  29.2 16.6 %fusion.63 = bf16[256,1024]{1,0:T(8,128)(2,1)S(1)} fusion(bf16[256,1024]{1,0:T(8,128)(2,1)S(1)} %get-tuple-element.79, f32[4096]{0:T(1024)S(1)} %maximum_select_fusion.6, f32[1024]{0:T(1024)S(1)} %maximum_select_fusion.11, f32[1024]{0:T(1024)S(1)} %get-tuple-element.65, f32[1024]{0:T(1024)S(1)} %get-tuple-element.68, f32[256]{0:T(256)S(1)} %add_rsqrt_fusion, ...), kind=kOutput, calls=%fused_computation.124 | convolution fusion | flops 4379377664 | bytes 17856512 | tf_op jit(solution)/shard_map/dot_general | solution.py:125
  45.8 5.0 %collective-permute-start.5 = (bf16[256,1024]{1,0:T(8,128)(2,1)S(1)}, bf16[256,1024]{1,0:T(8,128)(2,1)S(1)}, u32[]{:S(2)}, u32[]{:S(2)}) collective-permute-start(bf16[256,1024]{1,0:T(8,128)(2,1)S(1)} %fusion.63), channel_id=1, source_target_pairs={{0,16},{8,24},{1,17},{9,25},{2,18},{10,26},{3,19},{11,27},{4,20},{... | collective-permute-start | bytes 1572872 | tf_op jit(solution)/shard_map/ppermute | solution.py:24
  52.1 9.9 %collective-permute-done.5 = bf16[256,1024]{1,0:T(8,128)(2,1)S(1)} collective-permute-done((bf16[256,1024]{1,0:T(8,128)(2,1)S(1)}, bf16[256,1024]{1,0:T(8,128)(2,1)S(1)}, u32[]{:S(2)}, u32[]{:S(2)}) %collective-permute-start.5) | collective-permute-done | bytes 524320 | tf_op jit(solution)/shard_map/ppermute | solution.py:24
  62.9 6.0 %fusion.13 = bf16[256,3072]{1,0:T(8,128)(2,1)S(1)} fusion(bf16[256,1024]{1,0:T(8,128)(2,1)S(1)} %fusion.84, f32[3072]{0:T(1024)S(1)} %pad_maximum_fusion.5, bf16[512,3072]{1,0:T(8,128)(2,1)} %collective-permute-done.1, bf16[512,3072]{1,0:T(8,128)(2,1)} %param.15, pred[]{:T(512)S(6)} %eq.25), kind=kOutput, calls=%fused_computation.38 | convolution fusion | flops 1640497152 | bytes 8400897 | tf_op jit(solution)/shard_map/dot_general | solution.py:73
  69.8 3.5 fusion.185
  73.3 2.8 convolution_convert_fusion.8
  76.1 2.7 convert_reduce_fusion.2
  79.4 9.0 %multiply_convert_fusion.2 = (bf16[256,4096]{1,0:T(8,128)(2,1)}, f32[256,4096]{1,0:T(8,128)}) fusion(f32[4096]{0:T(1024)S(1)} %maximum_select_fusion.6, bf16[256,1024]{1,0:T(8,128)(2,1)S(1)} %fusion.81, bf16[512,4096]{1,0:T(8,128)(2,1)} %collective-permute-done.3, bf16[512,4096]{1,0:T(8,128)(2,1)S(1)} %copy-done.41, pred[]{:T(512)S(6)} %eq.25), kind=kOutput, calls=%fused_computation.27 | convolution fusion | flops 2191523840 | bytes 15220737 | tf_op jit(solution)/shard_map/dot_general | solution.py:121
  88.5 18.1 %fusion.100 = (f32[256]{0:T(256)S(1)}, f32[256,1024]{1,0:T(8,128)S(1)}) fusion(bf16[256,1024]{1,0:T(8,128)(2,1)S(1)} %get-tuple-element.83, f32[256]{0:T(256)S(1)} %broadcast_multiply_fusion, f32[1024]{0:T(1024)S(1)} %get-tuple-element.68, bf16[512,4096]{1,0:T(8,128)(2,1)} %collective-permute-done.3, bf16[512,4096]{1,0:T(8,128)(2,1)} %param.19, ...), kind=kOutput, calls=%fused_computation.166 | convolution fusion | flops 4384358400 | bytes 23076352 | tf_op jit(solution)/shard_map/dot_general | solution.py:134
  107.0 1.5 add_convert_fusion.8
  109.3 2.6 convolution_convert_fusion.7
  112.1 3.9 convolution_convert_fusion.6
  120.3 8.2 %fusion.97 = (f32[256]{0:T(256)S(1)}, f32[256,1024]{1,0:T(8,128)S(1)}) fusion(bf16[256,1024]{1,0:T(8,128)(2,1)S(1)} %get-tuple-element.31, f32[256]{0:T(256)S(1)} %broadcast_multiply_fusion.1, f32[1024]{0:T(1024)S(1)} %get-tuple-element.67, bf16[512,3072]{1,0:T(8,128)(2,1)} %collective-permute-done.1, bf16[512,3072]{1,0:T(8,128)(2,1)} %param.15, ...), kind=kOutput, calls=%fused_computation.163 | convolution fusion | flops 1644953344 | bytes 9443329 | tf_op jit(solution)/shard_map/dot_general | solution.py:113
  132.3 3.5 reshape.480
  135.8 8.7 %fusion.64 = bf16[256,1024]{1,0:T(8,128)(2,1)} fusion(bf16[256,4096]{1,0:T(8,128)(2,1)} %get-tuple-element.94, bf16[256,1024]{1,0:T(8,128)(2,1)S(1)} %get-tuple-element.83, f32[1024]{0:T(1024)S(1)} %maximum_select_fusion.11, bf16[2048,1024]{1,0:T(8,128)(2,1)} %collective-permute-done.4, bf16[2048,1024]{1,0:T(8,128)(2,1)} %param.21, pred[]{:T(512)S(6)} %eq.25), kind=kOutput, calls=%fused_computation.125 | convolution fusion | flops 2186280960 | bytes 11538433 | tf_op jit(solution)/shard_map/dot_general | solution.py:125
  144.5 2.2 reshape.470
  146.7 3.4 constant_dynamic-slice_fusion.11
  150.1 6.3 %constant_dynamic-slice_fusion.2 = (bf16[256,1,2048]{2,1,0:T(2,128)(2,1)}, bf16[256,1,2048]{2,1,0:T(2,128)(2,1)}) fusion(bf16[256,2,2048]{2,1,0:T(2,128)(2,1)S(1)} %reshape.480, s32[]{:T(128)S(6)} %select_n.331, s32[]{:T(128)S(6)} %select_n.355), kind=kLoop, calls=%fused_computation.252 | loop fusion | bytes 4194312 | tf_op jit(solution)/shard_map/jit(dynamic_index_in_dim)/dynamic_slice | solution.py:32
  157.6 14.4 %convert_reduce_fusion = (f32[4096]{0:T(1024)S(1)}, bf16[256,4096]{1,0:T(8,128)(2,1)S(1)}) fusion(f32[256,4096]{1,0:T(8,128)} %get-tuple-element.95, bf16[256,1024]{1,0:T(8,128)(2,1)S(1)} %get-tuple-element.21, bf16[2048,1024]{1,0:T(8,128)(2,1)} %collective-permute-done.4, bf16[2048,1024]{1,0:T(8,128)(2,1)} %param.21, pred[]{:T(512)S(6)} %eq.25), kind=kOutput, calls=%fused_computation.22 | convolution fusion | flops 2199908352 | bytes 15220737 | tf_op jit(solution)/shard_map/dot_general | solution.py:132
  172.0 8.8 %fusion.171 = (f32[1024]{0:T(1024)S(1)}, f32[256]{0:T(256)S(1)}, f32[256,1024]{1,0:T(8,128)S(1)}) fusion(f32[1024]{0:T(1024)S(1)} %get-tuple-element.68, f32[256]{0:T(256)S(1)} %broadcast_multiply_fusion, bf16[256,1024]{1,0:T(8,128)(2,1)S(1)} %get-tuple-element.83, bf16[256,4096]{1,0:T(8,128)(2,1)S(1)} %get-tuple-element.97, ...), kind=kOutput, calls=%fused_computation.330 | convolution fusion | flops 2186803968 | bytes 12068865 | tf_op jit(solution)/shard_map/dot_general | solution.py:134
  182.7 2.6 convolution_convert_fusion.5
  185.5 3.1 convolution_convert_fusion.4
  193.1 9.0 %fusion.170 = (f32[1024]{0:T(1024)S(1)}, f32[256]{0:T(256)S(1)}, f32[256,1024]{1,0:T(8,128)S(1)}) fusion(f32[1024]{0:T(1024)S(1)} %get-tuple-element.67, f32[256]{0:T(256)S(1)} %broadcast_multiply_fusion.1, bf16[256,1024]{1,0:T(8,128)(2,1)S(1)} %get-tuple-element.31, bf16[256,3072]{0,1:T(8,128)(2,1)S(1)} %get-tuple-element.25, ...), kind=kOutput, calls=%fused_computation.329 | convolution fusion | flops 1640495872 | bytes 9447425 | tf_op jit(solution)/shard_map/dot_general | solution.py:113
  203.9 2.4 collective-permute-start.7
  208.0 1.8 copy.153
  209.8 1.9 copy.154
  213.1 1.6 copy.149
  215.0 1.6 copy.150
  217.1 37.4 %all-reduce = f32[6144]{0:T(1024)S(1)} all-reduce(f32[6144]{0:T(1024)S(1)} %reshape.476), channel_id=2, replica_groups=mesh['section'=4,'dp'=8] {'dp'}, use_global_device_ids=true, to_apply=%region_30.31.clone | all-reduce | flops 6144 | bytes 49152
  262.6 1.9 convolution_convert_fusion.3
  264.9 3.7 convolution_convert_fusion.2
  269.4 1.7 collective-permute-start.35
  271.2 9.2 %convolution_convert_fusion.1 = bf16[512,3072]{1,0:T(8,128)(2,1)S(1)} fusion(bf16[256,3072]{0,1:T(8,128)(2,1)S(1)} %collective-permute-done.11, bf16[256,1024]{0,1:T(8,128)(2,1)S(1)} %bitcast.246, bf16[256,1024]{0,1:T(8,128)(2,1)S(1)} %bitcast.224, bf16[256,1024]{0,1:T(8,128)(2,1)S(1)} %bitcast.226, bf16[256,512]{1,0:T(8,128)(2,1)S(1)} %collective-permute-done.10, ...), kind=kOutput, calls=%fused_computation.13 | convolution fusion | flops 1625817088 | bytes 6815744 | tf_op jit(solution)/shard_map/dot_general | solution.py:139
  280.9 1.9 collective-permute-start.18
  283.0 12.1 %collective-permute-done.39 = bf16[4,256,512]{2,1,0:T(8,128)(2,1)S(1)} collective-permute-done((bf16[4,256,512]{2,1,0:T(8,128)(2,1)S(1)}, bf16[4,256,512]{2,1,0:T(8,128)(2,1)S(1)}, u32[]{:S(2)}, u32[]{:S(2)}) %collective-permute-start.39) | collective-permute-done | bytes 1048608 | tf_op jit(solution)/shard_map/ppermute | solution.py:28
  295.5 1.3 collective-permute-start.40
  296.9 2.4 convolution_convert_fusion
  300.0 2.1 collective-permute-start.29
  302.1 3.3 collective-permute-done.35
  305.5 1.9 collective-permute-start.25
  307.7 14.3 %collective-permute-done.40 = bf16[3,256,512]{2,1,0:T(8,128)(2,1)S(1)} collective-permute-done((bf16[3,256,512]{2,1,0:T(8,128)(2,1)S(1)}, bf16[3,256,512]{2,1,0:T(8,128)(2,1)S(1)}, u32[]{:S(2)}, u32[]{:S(2)}) %collective-permute-start.40) | collective-permute-done | bytes 786464 | tf_op jit(solution)/shard_map/ppermute | solution.py:49
  324.1 16.0 %collective-permute-done.12 = bf16[4,64,2048]{2,1,0:T(8,128)(2,1)S(1)} collective-permute-done((bf16[4,64,2048]{2,1,0:T(8,128)(2,1)S(1)}, bf16[4,64,2048]{2,1,0:T(8,128)(2,1)S(1)}, u32[]{:S(2)}, u32[]{:S(2)}) %collective-permute-start.12) | collective-permute-done | bytes 1048608 | tf_op jit(solution)/shard_map/ppermute | solution.py:28
  340.1 1.3 collective-permute-start.19
  341.9 22.5 %collective-permute-start.13 = (bf16[3,64,2048]{2,1,0:T(8,128)(2,1)S(1)}, bf16[3,64,2048]{2,1,0:T(8,128)(2,1)S(1)}, u32[]{:S(2)}, u32[]{:S(2)}) collective-permute-start(bf16[3,64,2048]{2,1,0:T(8,128)(2,1)S(1)} %constant_dynamic-slice_fusion.9), channel_id=1, source_target_pairs={{0,2},{1,3},{6,4},{7,5},{8,10},{9,11},{14,12},{15,13},{16,18},{17,... | collective-permute-start | bytes 2359304 | tf_op jit(solution)/shard_map/ppermute | solution.py:49
  364.5 1.3 collective-permute-start.42
  366.3 18.1 %collective-permute-done.25 = bf16[4,64,2048]{2,1,0:T(8,128)(2,1)S(1)} collective-permute-done((bf16[4,64,2048]{2,1,0:T(8,128)(2,1)S(1)}, bf16[4,64,2048]{2,1,0:T(8,128)(2,1)S(1)}, u32[]{:S(2)}, u32[]{:S(2)}) %collective-permute-start.25) | collective-permute-done | bytes 1048608 | tf_op jit(solution)/shard_map/ppermute | solution.py:28
  384.4 1.3 collective-permute-start.30
  386.2 1.6 collective-permute-start.26
  388.0 1.3 collective-permute-start.37
  391.1 12.0 %collective-permute-done.37 = bf16[1,2,256,512]{3,2,1,0:T(8,128)(2,1)S(1)} collective-permute-done((bf16[1,2,256,512]{3,2,1,0:T(8,128)(2,1)S(1)}, bf16[1,2,256,512]{3,2,1,0:T(8,128)(2,1)S(1)}, u32[]{:S(2)}, u32[]{:S(2)}) %collective-permute-start.37) | collective-permute-done | bytes 524320 | tf_op jit(solution)/shard_map/ppermute | solution.py:49
  405.0 14.2 %collective-permute-done.26 = bf16[3,64,2048]{2,1,0:T(8,128)(2,1)S(1)} collective-permute-done((bf16[3,64,2048]{2,1,0:T(8,128)(2,1)S(1)}, bf16[3,64,2048]{2,1,0:T(8,128)(2,1)S(1)}, u32[]{:S(2)}, u32[]{:S(2)}) %collective-permute-start.26) | collective-permute-done | bytes 786464 | tf_op jit(solution)/shard_map/ppermute | solution.py:49
  420.1 1.3 collective-permute-start.21
  421.5 1.3 collective-permute-start.15
  424.0 8.4 %collective-permute-done.21 = bf16[1,64,2048]{2,1,0:T(8,128)(2,1)S(1)} collective-permute-done((bf16[1,64,2048]{2,1,0:T(8,128)(2,1)S(1)}, bf16[1,64,2048]{2,1,0:T(8,128)(2,1)S(1)}, u32[]{:S(2)}, u32[]{:S(2)}) %collective-permute-start.21) | collective-permute-done | bytes 262176 | tf_op jit(solution)/shard_map/ppermute | solution.py:49
  433.2 2.9 collective-permute-done.15
  436.3 1.3 collective-permute-start.32
  438.6 1.3 collective-permute-start.28
  439.9 7.5 %collective-permute-done.32 = bf16[1,64,2048]{2,1,0:T(8,128)(2,1)S(1)} collective-permute-done((bf16[1,64,2048]{2,1,0:T(8,128)(2,1)S(1)}, bf16[1,64,2048]{2,1,0:T(8,128)(2,1)S(1)}, u32[]{:S(2)}, u32[]{:S(2)}) %collective-permute-start.32) | collective-permute-done | bytes 262176 | tf_op jit(solution)/shard_map/ppermute | solution.py:49
  447.6 2.7 collective-permute-done.28
  (310 shorter events, 60.9 us)
Async XLA Ops:
  0.6 6.9 %copy-start = (s32[2,256]{1,0:T(2,128)S(1)}, s32[2,256]{1,0:T(2,128)}, u32[]{:S(2)}) copy-start(s32[2,256]{1,0:T(2,128)} %param.14) | copy-start | bytes 6148
  0.7 12.0 %collective-permute-start.1 = (bf16[512,3072]{1,0:T(8,128)(2,1)}, bf16[512,3072]{1,0:T(8,128)(2,1)}, u32[]{:S(2)}, u32[]{:S(2)}) collective-permute-start(bf16[512,3072]{1,0:T(8,128)(2,1)} %param.15), channel_id=1, source_target_pairs={{0,8},{8,0},{16,24},{24,16},{1,9},{9,1},{17,25},{25,17},{2,10},{10... | collective-permute-start | bytes 9437192 | tf_op jit(solution)/shard_map/ppermute | solution.py:20
  5.3 6.4 %collective-permute-start = (f32[6144]{0:T(1024)S(1)}, f32[6144]{0:T(1024)S(1)}, u32[]{:S(2)}, u32[]{:S(2)}) collective-permute-start(f32[6144]{0:T(1024)S(1)} %constant_dynamic-update-slice_fusion), channel_id=1, source_target_pairs={{0,8},{8,0},{16,24},{24,16},{1,9},{9,1},{17,25},{25,17},{2,10},{10... | collective-permute-start | bytes 73736 | tf_op jit(solution)/shard_map/ppermute | solution.py:20
  5.4 20.8 %collective-permute-start.2 = (bf16[512,1024]{1,0:T(8,128)(2,1)}, bf16[512,1024]{1,0:T(8,128)(2,1)}, u32[]{:S(2)}, u32[]{:S(2)}) collective-permute-start(bf16[512,1024]{1,0:T(8,128)(2,1)} %param.17), channel_id=1, source_target_pairs={{0,8},{8,0},{16,24},{24,16},{1,9},{9,1},{17,25},{25,17},{2,10},{10... | collective-permute-start | bytes 3145736 | tf_op jit(solution)/shard_map/ppermute | solution.py:20
  5.8 23.3 %collective-permute-start.4 = (bf16[2048,1024]{1,0:T(8,128)(2,1)}, bf16[2048,1024]{1,0:T(8,128)(2,1)}, u32[]{:S(2)}, u32[]{:S(2)}) collective-permute-start(bf16[2048,1024]{1,0:T(8,128)(2,1)} %param.21), channel_id=1, source_target_pairs={{0,8},{8,0},{16,24},{24,16},{1,9},{9,1},{17,25},{25,17},{2,10},{10... | collective-permute-start | bytes 12582920 | tf_op jit(solution)/shard_map/ppermute | solution.py:20
  5.9 23.3 %collective-permute-start.3 = (bf16[512,4096]{1,0:T(8,128)(2,1)}, bf16[512,4096]{1,0:T(8,128)(2,1)}, u32[]{:S(2)}, u32[]{:S(2)}) collective-permute-start(bf16[512,4096]{1,0:T(8,128)(2,1)} %param.19), channel_id=1, source_target_pairs={{0,8},{8,0},{16,24},{24,16},{1,9},{9,1},{17,25},{25,17},{2,10},{10... | collective-permute-start | bytes 12582920 | tf_op jit(solution)/shard_map/ppermute | solution.py:20
  29.2 21.7 %copy-start.49 = (u32[32]{0:T(128)S(1)}, u32[32]{0:T(128)}, u32[]{:S(2)}) copy-start(u32[32]{0:T(128)} %constant.255) | copy-start | bytes 388
  45.8 16.2 %collective-permute-start.5 = (bf16[256,1024]{1,0:T(8,128)(2,1)S(1)}, bf16[256,1024]{1,0:T(8,128)(2,1)S(1)}, u32[]{:S(2)}, u32[]{:S(2)}) collective-permute-start(bf16[256,1024]{1,0:T(8,128)(2,1)S(1)} %fusion.63), channel_id=1, source_target_pairs={{0,16},{8,24},{1,17},{9,25},{2,18},{10,26},{3,19},{11,27},{4,20},{... | collective-permute-start | bytes 1572872 | tf_op jit(solution)/shard_map/ppermute | solution.py:24
  69.5 48.3 %copy-start.7 = (bf16[256,1024]{0,1:T(8,128)(2,1)}, bf16[256,1024]{0,1:T(8,128)(2,1)S(1)}, u32[]{:S(2)}) copy-start(bf16[256,1024]{0,1:T(8,128)(2,1)S(1)} %copy.90) | copy-start | bytes 1572868
  69.7 48.8 %copy-start.9 = (bf16[256,1024]{0,1:T(8,128)(2,1)}, bf16[256,1024]{0,1:T(8,128)(2,1)S(1)}, u32[]{:S(2)}) copy-start(bf16[256,1024]{0,1:T(8,128)(2,1)S(1)} %copy.91) | copy-start | bytes 1572868
  79.4 9.0 %copy-start.19 = (bf16[256,1024]{1,0:T(8,128)(2,1)}, bf16[256,1024]{1,0:T(8,128)(2,1)S(1)}, u32[]{:S(2)}) copy-start(bf16[256,1024]{1,0:T(8,128)(2,1)S(1)} %fusion.81) | copy-start | bytes 1572868
  120.3 8.6 %copy-start.22 = (bf16[256,1024]{1,0:T(8,128)(2,1)S(1)}, bf16[256,1024]{1,0:T(8,128)(2,1)}, u32[]{:S(2)}) copy-start(bf16[256,1024]{1,0:T(8,128)(2,1)} %copy-done.21) | copy-start | bytes 1572868
  130.1 26.2 %collective-permute-start.6 = (bf16[256,1024]{1,0:T(8,128)(2,1)}, bf16[256,1024]{1,0:T(8,128)(2,1)}, u32[]{:S(2)}, u32[]{:S(2)}) collective-permute-start(bf16[256,1024]{1,0:T(8,128)(2,1)} %add_convert_fusion.7), channel_id=1, source_target_pairs={{16,0},{24,8},{17,1},{25,9},{18,2},{26,10},{19,3},{27,11},{20,4},{... | collective-permute-start | bytes 1572872 | tf_op jit(solution)/shard_map/ppermute | solution.py:24
  132.3 129.9 %collective-permute-start.16 = (bf16[256,512]{0,1:T(8,128)(2,1)}, bf16[256,512]{0,1:T(8,128)(2,1)}, u32[]{:S(2)}, u32[]{:S(2)}) collective-permute-start(bf16[256,512]{0,1:T(8,128)(2,1)} %get-tuple-element.51), channel_id=1, source_target_pairs={{0,8},{8,0},{16,24},{24,16},{1,9},{9,1},{17,25},{25,17},{2,10},{10... | collective-permute-start | bytes 786440 | tf_op jit(solution)/shard_map/ppermute | solution.py:20
  157.6 23.8 %copy-start.15 = (bf16[256,1024]{1,0:T(8,128)(2,1)}, bf16[256,1024]{1,0:T(8,128)(2,1)S(1)}, u32[]{:S(2)}) copy-start(bf16[256,1024]{1,0:T(8,128)(2,1)S(1)} %get-tuple-element.21) | copy-start | bytes 1572868
  171.9 8.8 %copy-start.43 = (bf16[256,4096]{1,0:T(8,128)(2,1)}, bf16[256,4096]{1,0:T(8,128)(2,1)S(1)}, u32[]{:S(2)}) copy-start(bf16[256,4096]{1,0:T(8,128)(2,1)S(1)} %get-tuple-element.97) | copy-start | bytes 6291460
  191.7 10.3 %copy-start.23 = (bf16[16,64,256]{2,1,0:T(8,128)(2,1)}, bf16[16,64,256]{2,1,0:T(8,128)(2,1)S(1)}, u32[]{:S(2)}) copy-start(bf16[16,64,256]{2,1,0:T(8,128)(2,1)S(1)} %fusion.70) | copy-start | bytes 1572868
  192.2 9.8 %copy-start.25 = (bf16[16,64,256]{2,1,0:T(8,128)(2,1)}, bf16[16,64,256]{2,1,0:T(8,128)(2,1)S(1)}, u32[]{:S(2)}) copy-start(bf16[16,64,256]{2,1,0:T(8,128)(2,1)S(1)} %fusion.69) | copy-start | bytes 1572868
  192.7 9.3 %copy-start.27 = (bf16[256,3072]{0,1:T(8,128)(2,1)}, bf16[256,3072]{0,1:T(8,128)(2,1)S(1)}, u32[]{:S(2)}) copy-start(bf16[256,3072]{0,1:T(8,128)(2,1)S(1)} %get-tuple-element.25) | copy-start | bytes 4718596
  193.1 9.6 %copy-start.13 = (bf16[256,1024]{1,0:T(8,128)(2,1)S(1)}, bf16[256,1024]{1,0:T(8,128)(2,1)}, u32[]{:S(2)}) copy-start(bf16[256,1024]{1,0:T(8,128)(2,1)} %copy-done.12) | copy-start | bytes 1572868
  202.7 10.5 %copy-start.5 = (bf16[256,1,2048]{2,1,0:T(2,128)(2,1)S(1)}, bf16[256,1,2048]{2,1,0:T(2,128)(2,1)}, u32[]{:S(2)}) copy-start(bf16[256,1,2048]{2,1,0:T(2,128)(2,1)} %get-tuple-element.37) | copy-start | bytes 3145732
  203.9 50.7 %collective-permute-start.7 = (bf16[256,512]{1,0:T(8,128)(2,1)S(1)}, bf16[256,512]{1,0:T(8,128)(2,1)}, u32[]{:S(2)}, u32[]{:S(2)}) collective-permute-start(bf16[256,512]{1,0:T(8,128)(2,1)S(1)} %slice_select_fusion.1), channel_id=1, source_target_pairs={{0,16},{8,24},{16,0},{24,8},{1,17},{9,25},{17,1},{25,9},{2,18},{10... | collective-permute-start | bytes 786440 | tf_op jit(solution)/shard_map/ppermute | solution.py:24
  206.6 8.4 %copy-start.4 = (bf16[256,1,2048]{2,1,0:T(2,128)(2,1)S(1)}, bf16[256,1,2048]{2,1,0:T(2,128)(2,1)}, u32[]{:S(2)}) copy-start(bf16[256,1,2048]{2,1,0:T(2,128)(2,1)} %get-tuple-element.36) | copy-start | bytes 3145732
  206.6 10.2 %collective-permute-start.22 = (f32[8,768]{1,0:T(8,128)S(1)}, f32[8,768]{1,0:T(8,128)S(1)}, u32[]{:S(2)}, u32[]{:S(2)}) collective-permute-start(f32[8,768]{1,0:T(8,128)S(1)} %dynamic-slice_bitcast_fusion.7), channel_id=1, source_target_pairs={{0,8},{8,0},{16,24},{24,16},{1,9},{9,1},{17,25},{25,17},{2,10},{10... | collective-permute-start | bytes 73736 | tf_op jit(solution)/shard_map/ppermute | solution.py:20
  209.8 6.8 %copy-start.14 = (bf16[256,1024]{1,0:T(8,128)(2,1)S(1)}, bf16[256,1024]{1,0:T(8,128)(2,1)}, u32[]{:S(2)}) copy-start(bf16[256,1024]{1,0:T(8,128)(2,1)} %copy-done.12) | copy-start | bytes 1572868
  209.8 7.0 %copy-start.16 = (bf16[256,1024]{1,0:T(8,128)(2,1)S(1)}, bf16[256,1024]{1,0:T(8,128)(2,1)}, u32[]{:S(2)}) copy-start(bf16[256,1024]{1,0:T(8,128)(2,1)} %copy-done.15) | copy-start | bytes 1572868
  214.7 50.2 %collective-permute-start.33 = (bf16[256,2048]{1,0:T(8,128)(2,1)}, bf16[256,2048]{1,0:T(8,128)(2,1)}, u32[]{:S(2)}, u32[]{:S(2)}) collective-permute-start(bf16[256,2048]{1,0:T(8,128)(2,1)} %bitcast.188), channel_id=1, source_target_pairs={{0,8},{8,0},{16,24},{24,16},{1,9},{9,1},{17,25},{25,17},{2,10},{10... | collective-permute-start | bytes 3145736 | tf_op jit(solution)/shard_map/ppermute | solution.py:20
  215.0 45.1 %copy-start.28 = (bf16[256,3072]{0,1:T(8,128)(2,1)S(1)}, bf16[256,3072]{0,1:T(8,128)(2,1)}, u32[]{:S(2)}) copy-start(bf16[256,3072]{0,1:T(8,128)(2,1)} %copy-done.27) | copy-start | bytes 4718596
  216.6 45.8 %collective-permute-start.17 = (bf16[256,1024]{1,0:T(8,128)(2,1)S(1)}, bf16[256,1024]{1,0:T(8,128)(2,1)}, u32[]{:S(2)}, u32[]{:S(2)}) collective-permute-start(bf16[256,1024]{1,0:T(8,128)(2,1)S(1)} %copy-done.14), channel_id=1, source_target_pairs={{0,8},{8,0},{16,24},{24,16},{1,9},{9,1},{17,25},{25,17},{2,10},{10... | collective-permute-start | bytes 1572872 | tf_op jit(solution)/shard_map/ppermute | solution.py:20
  216.8 47.7 %collective-permute-start.34 = (bf16[256,1024]{1,0:T(8,128)(2,1)S(1)}, bf16[256,1024]{1,0:T(8,128)(2,1)}, u32[]{:S(2)}, u32[]{:S(2)}) collective-permute-start(bf16[256,1024]{1,0:T(8,128)(2,1)S(1)} %copy-done.16), channel_id=1, source_target_pairs={{0,8},{8,0},{16,24},{24,16},{1,9},{9,1},{17,25},{25,17},{2,10},{10... | collective-permute-start | bytes 1572872 | tf_op jit(solution)/shard_map/ppermute | solution.py:20
  257.1 1.6 collective-permute-start.8
  257.7 6.9 %copy-start.44 = (bf16[256,4096]{1,0:T(8,128)(2,1)S(1)}, bf16[256,4096]{1,0:T(8,128)(2,1)}, u32[]{:S(2)}) copy-start(bf16[256,4096]{1,0:T(8,128)(2,1)} %copy-done.43) | copy-start | bytes 6291460
  257.7 7.2 %copy-start.29 = (bf16[256,1,2048]{2,0,1:T(8,128)(2,1)S(1)}, bf16[256,1,2048]{2,0,1:T(8,128)(2,1)}, u32[]{:S(2)}) copy-start(bf16[256,1,2048]{2,0,1:T(8,128)(2,1)} %copy.150) | copy-start | bytes 3145732
  258.6 1.5 collective-permute-start.9
  260.1 11.0 %collective-permute-start.11 = (bf16[256,3072]{0,1:T(8,128)(2,1)S(1)}, bf16[256,3072]{0,1:T(8,128)(2,1)S(1)}, u32[]{:S(2)}, u32[]{:S(2)}) collective-permute-start(bf16[256,3072]{0,1:T(8,128)(2,1)S(1)} %copy-done.28), channel_id=1, source_target_pairs={{0,8},{8,0},{16,24},{24,16},{1,9},{9,1},{17,25},{25,17},{2,10},{10... | collective-permute-start | bytes 4718600 | tf_op jit(solution)/shard_map/ppermute | solution.py:20
  262.1 7.2 %collective-permute-start.10 = (bf16[256,512]{1,0:T(8,128)(2,1)}, bf16[256,512]{1,0:T(8,128)(2,1)S(1)}, u32[]{:S(2)}, u32[]{:S(2)}) collective-permute-start(bf16[256,512]{1,0:T(8,128)(2,1)} %bitcast.252), channel_id=1, source_target_pairs={{0,8},{8,0},{16,24},{24,16},{1,9},{9,1},{17,25},{25,17},{2,10},{10... | collective-permute-start | bytes 786440 | tf_op jit(solution)/shard_map/ppermute | solution.py:20
  262.3 33.2 %collective-permute-start.23 = (bf16[256,512]{1,0:T(8,128)(2,1)}, bf16[256,512]{1,0:T(8,128)(2,1)S(1)}, u32[]{:S(2)}, u32[]{:S(2)}) collective-permute-start(bf16[256,512]{1,0:T(8,128)(2,1)} %bitcast.250), channel_id=1, source_target_pairs={{0,8},{8,0},{16,24},{24,16},{1,9},{9,1},{17,25},{25,17},{2,10},{10... | collective-permute-start | bytes 786440 | tf_op jit(solution)/shard_map/ppermute | solution.py:20
  264.6 32.3 %collective-permute-start.24 = (bf16[256,4096]{1,0:T(8,128)(2,1)S(1)}, bf16[256,4096]{1,0:T(8,128)(2,1)S(1)}, u32[]{:S(2)}, u32[]{:S(2)}) collective-permute-start(bf16[256,4096]{1,0:T(8,128)(2,1)S(1)} %copy-done.44), channel_id=1, source_target_pairs={{0,8},{8,0},{16,24},{24,16},{1,9},{9,1},{17,25},{25,17},{2,10},{10... | collective-permute-start | bytes 6291464 | tf_op jit(solution)/shard_map/ppermute | solution.py:20
  269.1 26.1 %collective-permute-start.39 = (bf16[4,256,512]{2,1,0:T(8,128)(2,1)S(1)}, bf16[4,256,512]{2,1,0:T(8,128)(2,1)S(1)}, u32[]{:S(2)}, u32[]{:S(2)}) collective-permute-start(bf16[4,256,512]{2,1,0:T(8,128)(2,1)S(1)} %dynamic-slice_bitcast_fusion), channel_id=1, source_target_pairs={{0,1},{1,0},{2,3},{3,2},{4,5},{5,4},{6,7},{7,6},{8,9},{9,8},{10,11... | collective-permute-start | bytes 3145736 | tf_op jit(solution)/shard_map/ppermute | solution.py:28
  269.4 36.1 %collective-permute-start.35 = (bf16[3,2,256,512]{3,2,1,0:T(8,128)(2,1)S(1)}, bf16[3,2,256,512]{3,2,1,0:T(8,128)(2,1)S(1)}, u32[]{:S(2)}, u32[]{:S(2)}) collective-permute-start(bf16[3,2,256,512]{3,2,1,0:T(8,128)(2,1)S(1)} %constant_dynamic-slice_fusion), channel_id=1, source_target_pairs={{0,2},{1,3},{6,4},{7,5},{8,10},{9,11},{14,12},{15,13},{16,18},{17,... | collective-permute-start | bytes 4718600 | tf_op jit(solution)/shard_map/ppermute | solution.py:49
  280.8 16.1 %copy-start.39 = (bf16[256,1,512]{2,0,1:T(8,128)(2,1)S(1)}, bf16[256,1,512]{2,0,1:T(8,128)(2,1)}, u32[]{:S(2)}) copy-start(bf16[256,1,512]{2,0,1:T(8,128)(2,1)} %copy.152) | copy-start | bytes 786436
  280.9 41.9 %collective-permute-start.18 = (bf16[4,64,2048]{2,1,0:T(8,128)(2,1)S(1)}, bf16[4,64,2048]{2,1,0:T(8,128)(2,1)S(1)}, u32[]{:S(2)}, u32[]{:S(2)}) collective-permute-start(bf16[4,64,2048]{2,1,0:T(8,128)(2,1)S(1)} %dynamic-slice_bitcast_fusion.3), channel_id=1, source_target_pairs={{0,1},{1,0},{2,3},{3,2},{4,5},{5,4},{6,7},{7,6},{8,9},{9,8},{10,11... | collective-permute-start | bytes 3145736 | tf_op jit(solution)/shard_map/ppermute | solution.py:28
  295.1 44.9 %collective-permute-start.12 = (bf16[4,64,2048]{2,1,0:T(8,128)(2,1)S(1)}, bf16[4,64,2048]{2,1,0:T(8,128)(2,1)S(1)}, u32[]{:S(2)}, u32[]{:S(2)}) collective-permute-start(bf16[4,64,2048]{2,1,0:T(8,128)(2,1)S(1)} %dynamic-slice_bitcast_fusion.4), channel_id=1, source_target_pairs={{0,1},{1,0},{2,3},{3,2},{4,5},{5,4},{6,7},{7,6},{8,9},{9,8},{10,11... | collective-permute-start | bytes 3145736 | tf_op jit(solution)/shard_map/ppermute | solution.py:28
  295.5 26.5 %collective-permute-start.40 = (bf16[3,256,512]{2,1,0:T(8,128)(2,1)S(1)}, bf16[3,256,512]{2,1,0:T(8,128)(2,1)S(1)}, u32[]{:S(2)}, u32[]{:S(2)}) collective-permute-start(bf16[3,256,512]{2,1,0:T(8,128)(2,1)S(1)} %constant_dynamic-slice_fusion.4), channel_id=1, source_target_pairs={{0,2},{1,3},{6,4},{7,5},{8,10},{9,11},{14,12},{15,13},{16,18},{17,... | collective-permute-start | bytes 2359304 | tf_op jit(solution)/shard_map/ppermute | solution.py:49
  300.0 64.5 %collective-permute-start.29 = (bf16[4,64,2048]{2,1,0:T(8,128)(2,1)S(1)}, bf16[4,64,2048]{2,1,0:T(8,128)(2,1)S(1)}, u32[]{:S(2)}, u32[]{:S(2)}) collective-permute-start(bf16[4,64,2048]{2,1,0:T(8,128)(2,1)S(1)} %dynamic-slice_bitcast_fusion.1), channel_id=1, source_target_pairs={{0,1},{1,0},{2,3},{3,2},{4,5},{5,4},{6,7},{7,6},{8,9},{9,8},{10,11... | collective-permute-start | bytes 3145736 | tf_op jit(solution)/shard_map/ppermute | solution.py:28
  305.5 78.9 %collective-permute-start.25 = (bf16[4,64,2048]{2,1,0:T(8,128)(2,1)S(1)}, bf16[4,64,2048]{2,1,0:T(8,128)(2,1)S(1)}, u32[]{:S(2)}, u32[]{:S(2)}) collective-permute-start(bf16[4,64,2048]{2,1,0:T(8,128)(2,1)S(1)} %dynamic-slice_bitcast_fusion.2), channel_id=1, source_target_pairs={{0,1},{1,0},{2,3},{3,2},{4,5},{5,4},{6,7},{7,6},{8,9},{9,8},{10,11... | collective-permute-start | bytes 3145736 | tf_op jit(solution)/shard_map/ppermute | solution.py:28
  322.0 64.2 %collective-permute-start.36 = (bf16[2,2,256,512]{3,2,1,0:T(8,128)(2,1)S(1)}, bf16[2,2,256,512]{3,2,1,0:T(8,128)(2,1)S(1)}, u32[]{:S(2)}, u32[]{:S(2)}) collective-permute-start(bf16[2,2,256,512]{3,2,1,0:T(8,128)(2,1)S(1)} %add_convert_fusion), channel_id=1, source_target_pairs={{2,4},{3,5},{4,2},{5,3},{10,12},{11,13},{12,10},{13,11},{18,20},{1... | collective-permute-start | bytes 3145736 | tf_op jit(solution)/shard_map/ppermute | solution.py:49
  322.9 19.0 %collective-permute-start.41 = (bf16[2,256,512]{2,1,0:T(8,128)(2,1)S(1)}, bf16[2,256,512]{2,1,0:T(8,128)(2,1)S(1)}, u32[]{:S(2)}, u32[]{:S(2)}) collective-permute-start(bf16[2,256,512]{2,1,0:T(8,128)(2,1)S(1)} %add_convert_fusion.1), channel_id=1, source_target_pairs={{2,4},{3,5},{4,2},{5,3},{10,12},{11,13},{12,10},{13,11},{18,20},{1... | collective-permute-start | bytes 1572872 | tf_op jit(solution)/shard_map/ppermute | solution.py:49
  340.1 49.3 %collective-permute-start.19 = (bf16[3,64,2048]{2,1,0:T(8,128)(2,1)S(1)}, bf16[3,64,2048]{2,1,0:T(8,128)(2,1)S(1)}, u32[]{:S(2)}, u32[]{:S(2)}) collective-permute-start(bf16[3,64,2048]{2,1,0:T(8,128)(2,1)S(1)} %constant_dynamic-slice_fusion.8), channel_id=1, source_target_pairs={{0,2},{1,3},{6,4},{7,5},{8,10},{9,11},{14,12},{15,13},{16,18},{17,... | collective-permute-start | bytes 2359304 | tf_op jit(solution)/shard_map/ppermute | solution.py:49
  341.9 48.4 %collective-permute-start.13 = (bf16[3,64,2048]{2,1,0:T(8,128)(2,1)S(1)}, bf16[3,64,2048]{2,1,0:T(8,128)(2,1)S(1)}, u32[]{:S(2)}, u32[]{:S(2)}) collective-permute-start(bf16[3,64,2048]{2,1,0:T(8,128)(2,1)S(1)} %constant_dynamic-slice_fusion.9), channel_id=1, source_target_pairs={{0,2},{1,3},{6,4},{7,5},{8,10},{9,11},{14,12},{15,13},{16,18},{17,... | collective-permute-start | bytes 2359304 | tf_op jit(solution)/shard_map/ppermute | solution.py:49
  364.5 23.5 %collective-permute-start.42 = (bf16[1,256,512]{2,1,0:T(8,128)(2,1)S(1)}, bf16[1,256,512]{2,1,0:T(8,128)(2,1)S(1)}, u32[]{:S(2)}, u32[]{:S(2)}) collective-permute-start(bf16[1,256,512]{2,1,0:T(8,128)(2,1)S(1)} %add_convert_fusion.9), channel_id=1, source_target_pairs={{4,6},{5,7},{2,0},{3,1},{12,14},{13,15},{10,8},{11,9},{20,22},{21,... | collective-permute-start | bytes 786440 | tf_op jit(solution)/shard_map/ppermute | solution.py:49
  384.4 19.8 %collective-permute-start.30 = (bf16[3,64,2048]{2,1,0:T(8,128)(2,1)S(1)}, bf16[3,64,2048]{2,1,0:T(8,128)(2,1)S(1)}, u32[]{:S(2)}, u32[]{:S(2)}) collective-permute-start(bf16[3,64,2048]{2,1,0:T(8,128)(2,1)S(1)} %constant_dynamic-slice_fusion.3), channel_id=1, source_target_pairs={{0,2},{1,3},{6,4},{7,5},{8,10},{9,11},{14,12},{15,13},{16,18},{17,... | collective-permute-start | bytes 2359304 | tf_op jit(solution)/shard_map/ppermute | solution.py:49
  386.2 33.0 %collective-permute-start.26 = (bf16[3,64,2048]{2,1,0:T(8,128)(2,1)S(1)}, bf16[3,64,2048]{2,1,0:T(8,128)(2,1)S(1)}, u32[]{:S(2)}, u32[]{:S(2)}) collective-permute-start(bf16[3,64,2048]{2,1,0:T(8,128)(2,1)S(1)} %constant_dynamic-slice_fusion.5), channel_id=1, source_target_pairs={{0,2},{1,3},{6,4},{7,5},{8,10},{9,11},{14,12},{15,13},{16,18},{17,... | collective-permute-start | bytes 2359304 | tf_op jit(solution)/shard_map/ppermute | solution.py:49
  388.0 15.2 %collective-permute-start.37 = (bf16[1,2,256,512]{3,2,1,0:T(8,128)(2,1)S(1)}, bf16[1,2,256,512]{3,2,1,0:T(8,128)(2,1)S(1)}, u32[]{:S(2)}, u32[]{:S(2)}) collective-permute-start(bf16[1,2,256,512]{3,2,1,0:T(8,128)(2,1)S(1)} %add_convert_fusion.2), channel_id=1, source_target_pairs={{4,6},{5,7},{2,0},{3,1},{12,14},{13,15},{10,8},{11,9},{20,22},{21,... | collective-permute-start | bytes 1572872 | tf_op jit(solution)/shard_map/ppermute | solution.py:49
  389.6 30.5 %collective-permute-start.20 = (bf16[2,64,2048]{2,1,0:T(8,128)(2,1)S(1)}, bf16[2,64,2048]{2,1,0:T(8,128)(2,1)S(1)}, u32[]{:S(2)}, u32[]{:S(2)}) collective-permute-start(bf16[2,64,2048]{2,1,0:T(8,128)(2,1)S(1)} %add_convert_fusion.5), channel_id=1, source_target_pairs={{2,4},{3,5},{4,2},{5,3},{10,12},{11,13},{12,10},{13,11},{18,20},{1... | collective-permute-start | bytes 1572872 | tf_op jit(solution)/shard_map/ppermute | solution.py:49
  390.4 31.0 %collective-permute-start.14 = (bf16[2,64,2048]{2,1,0:T(8,128)(2,1)S(1)}, bf16[2,64,2048]{2,1,0:T(8,128)(2,1)S(1)}, u32[]{:S(2)}, u32[]{:S(2)}) collective-permute-start(bf16[2,64,2048]{2,1,0:T(8,128)(2,1)S(1)} %add_convert_fusion.6), channel_id=1, source_target_pairs={{2,4},{3,5},{4,2},{5,3},{10,12},{11,13},{12,10},{13,11},{18,20},{1... | collective-permute-start | bytes 1572872 | tf_op jit(solution)/shard_map/ppermute | solution.py:49
  403.5 19.4 %collective-permute-start.38 = (bf16[256,512]{1,0:T(8,128)(2,1)S(1)}, bf16[256,512]{1,0:T(8,128)(2,1)S(1)}, u32[]{:S(2)}, u32[]{:S(2)}) collective-permute-start(bf16[256,512]{1,0:T(8,128)(2,1)S(1)} %fusion.142), channel_id=1, source_target_pairs={{0,1},{1,0},{2,3},{3,2},{4,5},{5,4},{6,7},{7,6},{8,9},{9,8},{10,11... | collective-permute-start | bytes 786440 | tf_op jit(solution)/shard_map/ppermute | solution.py:28
  404.3 31.9 %collective-permute-start.31 = (bf16[2,64,2048]{2,1,0:T(8,128)(2,1)S(1)}, bf16[2,64,2048]{2,1,0:T(8,128)(2,1)S(1)}, u32[]{:S(2)}, u32[]{:S(2)}) collective-permute-start(bf16[2,64,2048]{2,1,0:T(8,128)(2,1)S(1)} %add_convert_fusion.3), channel_id=1, source_target_pairs={{2,4},{3,5},{4,2},{5,3},{10,12},{11,13},{12,10},{13,11},{18,20},{1... | collective-permute-start | bytes 1572872 | tf_op jit(solution)/shard_map/ppermute | solution.py:49
  419.3 19.2 %collective-permute-start.27 = (bf16[2,64,2048]{2,1,0:T(8,128)(2,1)S(1)}, bf16[2,64,2048]{2,1,0:T(8,128)(2,1)S(1)}, u32[]{:S(2)}, u32[]{:S(2)}) collective-permute-start(bf16[2,64,2048]{2,1,0:T(8,128)(2,1)S(1)} %add_convert_fusion.4), channel_id=1, source_target_pairs={{2,4},{3,5},{4,2},{5,3},{10,12},{11,13},{12,10},{13,11},{18,20},{1... | collective-permute-start | bytes 1572872 | tf_op jit(solution)/shard_map/ppermute | solution.py:49
  420.1 12.2 %collective-permute-start.21 = (bf16[1,64,2048]{2,1,0:T(8,128)(2,1)S(1)}, bf16[1,64,2048]{2,1,0:T(8,128)(2,1)S(1)}, u32[]{:S(2)}, u32[]{:S(2)}) collective-permute-start(bf16[1,64,2048]{2,1,0:T(8,128)(2,1)S(1)} %add_convert_fusion.12), channel_id=1, source_target_pairs={{4,6},{5,7},{2,0},{3,1},{12,14},{13,15},{10,8},{11,9},{20,22},{21,... | collective-permute-start | bytes 786440 | tf_op jit(solution)/shard_map/ppermute | solution.py:49
  421.5 14.5 %collective-permute-start.15 = (bf16[1,64,2048]{2,1,0:T(8,128)(2,1)S(1)}, bf16[1,64,2048]{2,1,0:T(8,128)(2,1)S(1)}, u32[]{:S(2)}, u32[]{:S(2)}) collective-permute-start(bf16[1,64,2048]{2,1,0:T(8,128)(2,1)S(1)} %add_convert_fusion.13), channel_id=1, source_target_pairs={{4,6},{5,7},{2,0},{3,1},{12,14},{13,15},{10,8},{11,9},{20,22},{21,... | collective-permute-start | bytes 786440 | tf_op jit(solution)/shard_map/ppermute | solution.py:49
  436.1 15.4 %copy-start.1 = (s32[2,256]{1,0:T(2,128)S(1)}, s32[2,256]{1,0:T(2,128)}, u32[]{:S(2)}) copy-start(s32[2,256]{1,0:T(2,128)} %param.14) | copy-start | bytes 6148
  436.3 11.1 %collective-permute-start.32 = (bf16[1,64,2048]{2,1,0:T(8,128)(2,1)S(1)}, bf16[1,64,2048]{2,1,0:T(8,128)(2,1)S(1)}, u32[]{:S(2)}, u32[]{:S(2)}) collective-permute-start(bf16[1,64,2048]{2,1,0:T(8,128)(2,1)S(1)} %add_convert_fusion.10), channel_id=1, source_target_pairs={{4,6},{5,7},{2,0},{3,1},{12,14},{13,15},{10,8},{11,9},{20,22},{21,... | collective-permute-start | bytes 786440 | tf_op jit(solution)/shard_map/ppermute | solution.py:49
  438.6 11.6 %collective-permute-start.28 = (bf16[1,64,2048]{2,1,0:T(8,128)(2,1)S(1)}, bf16[1,64,2048]{2,1,0:T(8,128)(2,1)S(1)}, u32[]{:S(2)}, u32[]{:S(2)}) collective-permute-start(bf16[1,64,2048]{2,1,0:T(8,128)(2,1)S(1)} %add_convert_fusion.11), channel_id=1, source_target_pairs={{4,6},{5,7},{2,0},{3,1},{12,14},{13,15},{10,8},{11,9},{20,22},{21,... | collective-permute-start | bytes 786440 | tf_op jit(solution)/shard_map/ppermute | solution.py:49
  (29 other events, 80.4 us)
